TPU v7x, 32 devices: a whole 2x2x4 slice. The times are simulated.
32 devices in a mesh: frame: 4 (over x, core), clip: 8 (over z, y).
Axes of the slice: x: 2, y: 2, z: 4, core: 2. Of those that a mesh axis runs over, the one named last changes fastest.
Arguments:
- within_frame_asker_matrix: bfloat16 [8, 4, 128, 1536], P('clip', 'frame'), may hold values from -400 to 400
- within_frame_matcher_matrix: bfloat16 [8, 4, 128, 1536], P('clip', 'frame'), may hold values from -6 to 6
- within_frame_payload_matrix: bfloat16 [8, 4, 128, 1536], P('clip', 'frame'), may hold values from -5 to 5
- within_frame_upstream_derivative: bfloat16 [8, 4, 128, 1536], P('clip', 'frame'), may hold values from -48 to 48
- across_time_asker_matrix: bfloat16 [8, 4, 128, 1536], P('clip', 'frame'), may hold values from -400 to 400
- across_time_matcher_matrix: bfloat16 [8, 4, 128, 1536], P('clip', 'frame'), may hold values from -6 to 6
- across_time_payload_matrix: bfloat16 [8, 4, 128, 1536], P('clip', 'frame'), may hold values from -5 to 5
- across_time_upstream_derivative: bfloat16 [8, 4, 128, 1536], P('clip', 'frame'), may hold values from -48 to 48
- sharpness_factor: float32 [2, 12], replicated, may hold values from 0.7 to 1.4
Outputs:
- spatial_query_grad: bfloat16 [8, 4, 128, 1536], P('clip', 'frame')
- spatial_key_grad: bfloat16 [8, 4, 128, 1536], P('clip', 'frame')
- temporal_query_grad: bfloat16 [8, 4, 128, 1536], P('clip', 'frame')
- temporal_key_grad: bfloat16 [8, 4, 128, 1536], P('clip', 'frame')
- temporal_value_grad: bfloat16 [8, 4, 128, 1536], P('clip', 'frame')
- logit_scale_gradient: float32 [2, 12], replicated
All inputs are finite; a program needn't handle non-finite values.
Results may differ from a plain program's by a relative error of at most 0.011.
Values may be sent and summed in bfloat16 or wider, within the bound.
A program may use at most 64 MiB of HBM per device.

v0:
```python
import math

import jax
import jax.numpy as jnp
from jax import lax
from jax.sharding import PartitionSpec as P


def softmax_mixing_reverse_pass(queries, key_rows, values, cotangent, temper_row, causal):
    head_width = queries.shape[-1]
    raw_scores = jnp.einsum(
        "lbhk,mbhk->bhlm", queries, key_rows, preferred_element_type=jnp.float32
    ) / math.sqrt(head_width)
    scores = temper_row[None, :, None, None] * raw_scores
    if causal:
        length = queries.shape[0]
        row_index = lax.broadcasted_iota(jnp.int32, (length, length), 0)
        col_index = lax.broadcasted_iota(jnp.int32, (length, length), 1)
        scores = jnp.where(col_index <= row_index, scores, -jnp.inf)
    row_max = jnp.max(scores, axis=-1, keepdims=True)
    exponent = jnp.exp(scores - row_max)
    soft_weights = exponent / jnp.sum(exponent, axis=-1, keepdims=True)
    weights_low = soft_weights.astype(jnp.bfloat16)
    value_grad = jnp.einsum(
        "bhlm,lbhk->mbhk", weights_low, cotangent, preferred_element_type=jnp.float32
    )
    weight_grad = jnp.einsum(
        "lbhk,mbhk->bhlm", cotangent, values, preferred_element_type=jnp.float32
    )
    row_delta = jnp.sum(soft_weights * weight_grad, axis=-1, keepdims=True)
    score_grad = soft_weights * (weight_grad - row_delta)
    score_low = score_grad.astype(jnp.bfloat16)
    factor = (temper_row / math.sqrt(head_width))[None, None, :, None]
    query_grad = (
        jnp.einsum("bhlm,mbhk->lbhk", score_low, key_rows, preferred_element_type=jnp.float32)
        * factor
    )
    key_grad = (
        jnp.einsum("bhlm,lbhk->mbhk", score_low, queries, preferred_element_type=jnp.float32)
        * factor
    )
    payload_derivative_share = jnp.sum(score_grad * raw_scores, axis=(2, 3))
    return (
        query_grad.astype(jnp.bfloat16),
        key_grad.astype(jnp.bfloat16),
        value_grad.astype(jnp.bfloat16),
        payload_derivative_share,
    )


def across_time_elements(pieces, temper_row, channel_bundle):
    frames = pieces[0].shape[0]
    count = pieces[0].shape[2]
    features = pieces[0].shape[3]
    shaped = [
        piece.reshape(frames, count, channel_bundle, features // channel_bundle) for piece in pieces
    ]
    grads = softmax_mixing_reverse_pass(
        shaped[0], shaped[1], shaped[2], shaped[3], temper_row, True
    )
    unrolled_vector = tuple((block.reshape(frames, 1, count, features) for block in grads[:3]))
    return (unrolled_vector, grads[3])


def on_device(
    within_frame_asker_matrix,
    within_frame_matcher_matrix,
    within_frame_payload_matrix,
    within_frame_upstream_derivative,
    across_time_asker_matrix,
    across_time_matcher_matrix,
    across_time_payload_matrix,
    across_time_upstream_derivative,
    sharpness_factor,
):
    channel_bundle = sharpness_factor.shape[1]
    patches = within_frame_asker_matrix.shape[2]
    features = within_frame_asker_matrix.shape[3]
    head_width = features // channel_bundle
    groups = lax.axis_size("frame")
    group_width = patches // groups

    def to_heads(block):
        return block.reshape(patches, 1, channel_bundle, head_width)

    def from_heads(block):
        return block.reshape(1, 1, patches, features)

    def to_groups(block):
        return block.reshape(1, groups, group_width, features)

    spatial_result = softmax_mixing_reverse_pass(
        to_heads(within_frame_asker_matrix),
        to_heads(within_frame_matcher_matrix),
        to_heads(within_frame_payload_matrix),
        to_heads(within_frame_upstream_derivative),
        sharpness_factor[0],
        False,
    )
    spatial_part = jnp.sum(spatial_result[3], axis=0)
    incoming_shards = (
        lax.all_to_all(
            to_groups(across_time_asker_matrix), "frame", split_axis=1, concat_axis=0, tiled=True
        ),
        lax.all_to_all(
            to_groups(across_time_matcher_matrix), "frame", split_axis=1, concat_axis=0, tiled=True
        ),
        lax.all_to_all(
            to_groups(across_time_payload_matrix), "frame", split_axis=1, concat_axis=0, tiled=True
        ),
        lax.all_to_all(
            to_groups(across_time_upstream_derivative),
            "frame",
            split_axis=1,
            concat_axis=0,
            tiled=True,
        ),
    )
    unrolled_vector, payload_derivative_share = across_time_elements(
        incoming_shards, sharpness_factor[1], channel_bundle
    )
    temporal_grads = (
        lax.all_to_all(unrolled_vector[0], "frame", split_axis=0, concat_axis=1, tiled=True),
        lax.all_to_all(unrolled_vector[1], "frame", split_axis=0, concat_axis=1, tiled=True),
        lax.all_to_all(unrolled_vector[2], "frame", split_axis=0, concat_axis=1, tiled=True),
    )
    temporal_part = jnp.sum(payload_derivative_share, axis=0)
    scale_norm = 1.0 / math.sqrt(
        lax.axis_size("clip")
        * within_frame_asker_matrix.shape[0]
        * groups
        * within_frame_asker_matrix.shape[1]
        * patches
    )
    summed_totals = lax.psum(jnp.stack([spatial_part, temporal_part]), ("frame", "clip"))
    logit_scale_gradient = summed_totals * scale_norm
    return (
        from_heads(spatial_result[0]),
        from_heads(spatial_result[1]),
        from_heads(temporal_grads[0]),
        from_heads(temporal_grads[1]),
        from_heads(temporal_grads[2]),
        logit_scale_gradient,
    )


def solution(mesh):
    return jax.shard_map(
        on_device,
        mesh=mesh,
        in_specs=(
            P("clip", "frame", None, None),
            P("clip", "frame", None, None),
            P("clip", "frame", None, None),
            P("clip", "frame", None, None),
            P("clip", "frame", None, None),
            P("clip", "frame", None, None),
            P("clip", "frame", None, None),
            P("clip", "frame", None, None),
            P(),
        ),
        out_specs=(
            P("clip", "frame", None, None),
            P("clip", "frame", None, None),
            P("clip", "frame", None, None),
            P("clip", "frame", None, None),
            P("clip", "frame", None, None),
            P(),
        ),
        check_vma=False,
    )
```

profile of v0, /device:TPU:0, one launch (start us, length us, event | category | flops | bytes accessed | tf_op | source)
XLA Modules:
  0.0 122.1 jit_solution(1534998817248992619)
XLA Ops:
  0.6 4.4 %all-to-all-start.1 = ((bf16[1,4,32,1536]{3,2,0,1:T(8,128)(2,1)}), bf16[1,4,32,1536]{3,2,0,1:T(8,128)(2,1)S(1)}, u32[]{:S(2)}, u32[]{:S(2)}) async-start(bf16[1,4,32,1536]{3,2,0,1:T(8,128)(2,1)} %bitcast.83), calls=%async_computation.1 | async-start | bytes 786432 | tf_op jit(solution)/shard_map/all_to_all | solution.py:105
  5.0 0.2 copy.50
  5.2 0.8 copy-done.4
  6.0 0.2 copy.49
  6.2 0.3 fusion.38
  6.6 0.3 copy-done.8
  6.9 0.5 multiply_bitcast_fusion
  7.4 0.9 copy.53
  8.4 0.9 copy.54
  9.3 1.5 %fusion.36 = (f32[12,128]{1,0:T(8,128)S(1)}, f32[12,128,128]{1,2,0:T(8,128)S(1)}) fusion(f32[12,128,128]{1,2,0:T(8,128)S(1)} %fusion.38, f32[12]{0:T(128)S(1)} %get-tuple-element.29), kind=kOutput, calls=%fused_computation.56 | output fusion | flops 589951 | bytes 1579056 | tf_op jit(solution)/shard_map/sub | solution.py:21
  10.8 1.6 %all-to-all-done.1 = bf16[1,4,32,1536]{3,2,0,1:T(8,128)(2,1)S(1)} async-done(((bf16[1,4,32,1536]{3,2,0,1:T(8,128)(2,1)}), bf16[1,4,32,1536]{3,2,0,1:T(8,128)(2,1)S(1)}, u32[]{:S(2)}, u32[]{:S(2)}) %all-to-all-start.1) | async-done | bytes 393248 | tf_op jit(solution)/shard_map/all_to_all | solution.py:105
  12.4 3.6 %all-to-all-start = ((bf16[1,4,32,1536]{3,2,0,1:T(8,128)(2,1)}), bf16[1,4,32,1536]{3,2,0,1:T(8,128)(2,1)S(1)}, u32[]{:S(2)}, u32[]{:S(2)}) async-start(bf16[1,4,32,1536]{3,2,0,1:T(8,128)(2,1)} %bitcast.13), calls=%async_computation | async-start | bytes 786432 | tf_op jit(solution)/shard_map/all_to_all | solution.py:102
  16.0 1.3 %multiply_reduce_fusion.3 = (f32[12,128]{1,0:T(8,128)S(1)}, f32[12,128,128]{1,2,0:T(8,128)S(1)}) fusion(f32[12,128,128]{1,2,0:T(8,128)S(1)} %get-tuple-element.31, f32[12,128]{1,0:T(8,128)S(1)} %get-tuple-element.30, bf16[128,12,128]{0,2,1:T(8,128)(2,1)S(1)} %bitcast.85, bf16[128,12,128]{0,2,1:T(8,128)(2,1)} %bitcast.86), kind=kOutput, calls=%fused_computation.26 | convolution fusion | flops 50919936 | bytes 2371584 | tf_op jit(solution)/shard_map/lbhk,mbhk->bhlm/dot_general | solution.py:27
  17.4 0.3 multiply_reduce_fusion.1
  17.7 5.7 %all-to-all-done = bf16[1,4,32,1536]{3,2,0,1:T(8,128)(2,1)S(1)} async-done(((bf16[1,4,32,1536]{3,2,0,1:T(8,128)(2,1)}), bf16[1,4,32,1536]{3,2,0,1:T(8,128)(2,1)S(1)}, u32[]{:S(2)}, u32[]{:S(2)}) %all-to-all-start) | async-done | bytes 393248 | tf_op jit(solution)/shard_map/all_to_all | solution.py:102
  23.4 3.5 %all-to-all-start.3 = ((bf16[1,4,32,1536]{3,2,0,1:T(8,128)(2,1)}), bf16[1,4,32,1536]{3,2,0,1:T(8,128)(2,1)S(1)}, u32[]{:S(2)}, u32[]{:S(2)}) async-start(bf16[1,4,32,1536]{3,2,0,1:T(8,128)(2,1)} %bitcast.84), calls=%async_computation.3 | async-start | bytes 786432 | tf_op jit(solution)/shard_map/all_to_all | solution.py:108
  26.9 0.3 fusion.8
  27.2 1.1 reshape.180
  28.3 1.1 reshape.178
  29.3 5.0 %all-to-all-done.3 = bf16[1,4,32,1536]{3,2,0,1:T(8,128)(2,1)S(1)} async-done(((bf16[1,4,32,1536]{3,2,0,1:T(8,128)(2,1)}), bf16[1,4,32,1536]{3,2,0,1:T(8,128)(2,1)S(1)}, u32[]{:S(2)}, u32[]{:S(2)}) %all-to-all-start.3) | async-done | bytes 393248 | tf_op jit(solution)/shard_map/all_to_all | solution.py:108
  34.3 3.5 %all-to-all-start.2 = ((bf16[1,4,32,1536]{3,2,0,1:T(8,128)(2,1)}), bf16[1,4,32,1536]{3,2,0,1:T(8,128)(2,1)S(1)}, u32[]{:S(2)}, u32[]{:S(2)}) async-start(bf16[1,4,32,1536]{3,2,0,1:T(8,128)(2,1)} %bitcast.16), calls=%async_computation.2 | async-start | bytes 786432 | tf_op jit(solution)/shard_map/all_to_all | solution.py:111
  37.8 1.8 %fusion.27 = f32[32,12,4,4]{2,3,1,0:T(4,128)S(1)} fusion(bf16[4,32,12,128]{3,2,1,0:T(8,128)(2,1)} %reshape.180, bf16[4,32,12,128]{3,2,1,0:T(8,128)(2,1)} %reshape.178), kind=kOutput, calls=%fused_computation.42 | convolution fusion | flops 1572864 | bytes 811008 | tf_op jit(solution)/shard_map/lbhk,mbhk->bhlm/dot_general | solution.py:11
  39.6 1.1 reshape.184
  40.7 0.7 copy-done.9
  41.3 1.2 fusion.37
  42.6 2.6 %all-to-all-done.2 = bf16[1,4,32,1536]{3,2,0,1:T(8,128)(2,1)S(1)} async-done(((bf16[1,4,32,1536]{3,2,0,1:T(8,128)(2,1)}), bf16[1,4,32,1536]{3,2,0,1:T(8,128)(2,1)S(1)}, u32[]{:S(2)}, u32[]{:S(2)}) %all-to-all-start.2) | async-done | bytes 393248 | tf_op jit(solution)/shard_map/all_to_all | solution.py:111
  45.2 1.1 reshape.182
  46.3 2.3 %multiply_reduce_fusion.2 = (f32[32,12,4]{2,1,0:T(8,128)S(1)}, f32[32,12,4,4]{2,3,1,0:T(4,128)S(1)}) fusion(f32[32,12,4,4]{2,3,1,0:T(4,128)S(1)} %get-tuple-element.35, f32[32,12,4]{2,1,0:T(8,128)S(1)} %get-tuple-element.34, bf16[4,32,12,128]{3,2,1,0:T(8,128)(2,1)} %reshape.184, bf16[4,32,12,128]{3,2,1,0:T(8,128)(2,1)} %reshape.182), kind=kOutput, calls=%fused_computation.23 | convolution fusion | flops 1589760 | bytes 847872 | tf_op jit(solution)/shard_map/lbhk,mbhk->bhlm/dot_general | solution.py:27
  48.6 0.8 multiply_reduce_fusion
  49.6 0.7 fusion.14
  50.4 1.0 reshape.185
  51.4 3.5 %all-to-all-start.4 = ((bf16[4,1,32,1536]{3,2,1,0:T(8,128)(2,1)}), bf16[4,1,32,1536]{3,2,1,0:T(8,128)(2,1)S(1)}, u32[]{:S(2)}, u32[]{:S(2)}) async-start(bf16[4,1,32,1536]{3,2,1,0:T(8,128)(2,1)} %bitcast.19), calls=%async_computation.4 | async-start | bytes 786432 | tf_op jit(solution)/shard_map/all_to_all | solution.py:123
  54.9 0.4 fusion.9
  55.3 0.9 copy.73
  56.4 0.5 fusion.13
  57.0 1.0 reshape.187
  58.0 4.3 %all-to-all-done.4 = bf16[4,1,32,1536]{3,2,1,0:T(8,128)(2,1)S(1)} async-done(((bf16[4,1,32,1536]{3,2,1,0:T(8,128)(2,1)}), bf16[4,1,32,1536]{3,2,1,0:T(8,128)(2,1)S(1)}, u32[]{:S(2)}, u32[]{:S(2)}) %all-to-all-start.4) | async-done | bytes 393248 | tf_op jit(solution)/shard_map/all_to_all | solution.py:123
  62.3 3.5 %all-to-all-start.5 = ((bf16[4,1,32,1536]{3,2,1,0:T(8,128)(2,1)}), bf16[4,1,32,1536]{3,2,1,0:T(8,128)(2,1)S(1)}, u32[]{:S(2)}, u32[]{:S(2)}) async-start(bf16[4,1,32,1536]{3,2,1,0:T(8,128)(2,1)} %bitcast.22), calls=%async_computation.5 | async-start | bytes 786432 | tf_op jit(solution)/shard_map/all_to_all | solution.py:124
  65.8 0.6 fusion.12
  66.5 1.0 reshape.189
  67.5 5.7 %all-to-all-done.5 = bf16[4,1,32,1536]{3,2,1,0:T(8,128)(2,1)S(1)} async-done(((bf16[4,1,32,1536]{3,2,1,0:T(8,128)(2,1)}), bf16[4,1,32,1536]{3,2,1,0:T(8,128)(2,1)S(1)}, u32[]{:S(2)}, u32[]{:S(2)}) %all-to-all-start.5) | async-done | bytes 393248 | tf_op jit(solution)/shard_map/all_to_all | solution.py:124
  73.2 3.5 %all-to-all-start.6 = ((bf16[4,1,32,1536]{3,2,1,0:T(8,128)(2,1)}), bf16[4,1,32,1536]{3,2,1,0:T(8,128)(2,1)S(1)}, u32[]{:S(2)}, u32[]{:S(2)}) async-start(bf16[4,1,32,1536]{3,2,1,0:T(8,128)(2,1)} %bitcast.25), calls=%async_computation.6 | async-start | bytes 786432 | tf_op jit(solution)/shard_map/all_to_all | solution.py:125
  76.7 0.9 copy.74
  77.6 41.7 %psum.7 = f32[2,12]{1,0:T(2,128)S(1)} all-reduce(f32[2,12]{1,0:T(2,128)S(1)} %pad_maximum_fusion), channel_id=1, replica_groups=mesh['frame'=4,'clip'=8] {'frame','clip'}, use_global_device_ids=true, to_apply=%region_8.9 | all-reduce | flops 24 | bytes 192 | tf_op jit(solution)/shard_map/psum | solution.py:135
  119.3 0.6 broadcast_multiply_fusion
  119.8 0.7 copy.103
  120.6 0.7 copy.104
  121.3 0.7 copy.105
  (23 shorter events, 0.7 us)
Async XLA Ops:
  0.6 4.4 %copy-start.3 = (bf16[1,1,128,1536]{3,2,1,0:T(8,128)(2,1)S(1)}, bf16[1,1,128,1536]{3,2,1,0:T(8,128)(2,1)}, u32[]{:S(2)}) copy-start(bf16[1,1,128,1536]{3,2,1,0:T(8,128)(2,1)} %param.10) | copy-start | bytes 1179652
  0.6 11.8 %all-to-all-start.1 = ((bf16[1,4,32,1536]{3,2,0,1:T(8,128)(2,1)}), bf16[1,4,32,1536]{3,2,0,1:T(8,128)(2,1)S(1)}, u32[]{:S(2)}, u32[]{:S(2)}) async-start(bf16[1,4,32,1536]{3,2,0,1:T(8,128)(2,1)} %bitcast.83), calls=%async_computation.1 | async-start | bytes 786432 | tf_op jit(solution)/shard_map/all_to_all | solution.py:105
  5.0 1.0 copy-start.4
  6.2 0.7 copy-start.8
  6.2 1.2 copy-start.5
  7.4 1.0 copy-start.6
  12.4 3.6 %copy-start.7 = (bf16[1,1,128,1536]{2,3,1,0:T(8,128)(2,1)S(1)}, bf16[1,1,128,1536]{2,3,1,0:T(8,128)(2,1)}, u32[]{:S(2)}) copy-start(bf16[1,1,128,1536]{2,3,1,0:T(8,128)(2,1)} %copy.53) | copy-start | bytes 1179652
  12.4 11.0 %all-to-all-start = ((bf16[1,4,32,1536]{3,2,0,1:T(8,128)(2,1)}), bf16[1,4,32,1536]{3,2,0,1:T(8,128)(2,1)S(1)}, u32[]{:S(2)}, u32[]{:S(2)}) async-start(bf16[1,4,32,1536]{3,2,0,1:T(8,128)(2,1)} %bitcast.13), calls=%async_computation | async-start | bytes 786432 | tf_op jit(solution)/shard_map/all_to_all | solution.py:102
  23.4 10.9 %all-to-all-start.3 = ((bf16[1,4,32,1536]{3,2,0,1:T(8,128)(2,1)}), bf16[1,4,32,1536]{3,2,0,1:T(8,128)(2,1)S(1)}, u32[]{:S(2)}, u32[]{:S(2)}) async-start(bf16[1,4,32,1536]{3,2,0,1:T(8,128)(2,1)} %bitcast.84), calls=%async_computation.3 | async-start | bytes 786432 | tf_op jit(solution)/shard_map/all_to_all | solution.py:108
  34.3 10.9 %all-to-all-start.2 = ((bf16[1,4,32,1536]{3,2,0,1:T(8,128)(2,1)}), bf16[1,4,32,1536]{3,2,0,1:T(8,128)(2,1)S(1)}, u32[]{:S(2)}, u32[]{:S(2)}) async-start(bf16[1,4,32,1536]{3,2,0,1:T(8,128)(2,1)} %bitcast.16), calls=%async_computation.2 | async-start | bytes 786432 | tf_op jit(solution)/shard_map/all_to_all | solution.py:111
  40.7 0.7 copy-start.9
  48.6 1.0 copy-start.2
  51.4 10.9 %all-to-all-start.4 = ((bf16[4,1,32,1536]{3,2,1,0:T(8,128)(2,1)}), bf16[4,1,32,1536]{3,2,1,0:T(8,128)(2,1)S(1)}, u32[]{:S(2)}, u32[]{:S(2)}) async-start(bf16[4,1,32,1536]{3,2,1,0:T(8,128)(2,1)} %bitcast.19), calls=%async_computation.4 | async-start | bytes 786432 | tf_op jit(solution)/shard_map/all_to_all | solution.py:123
  55.3 1.0 copy-start
  58.0 7.8 %copy-start.1 = (bf16[4,32,12,128]{3,2,1,0:T(8,128)(2,1)S(1)}, bf16[4,32,12,128]{3,2,1,0:T(8,128)(2,1)}, u32[]{:S(2)}) copy-start(bf16[4,32,12,128]{3,2,1,0:T(8,128)(2,1)} %reshape.182) | copy-start | bytes 1179652
  62.3 10.9 %all-to-all-start.5 = ((bf16[4,1,32,1536]{3,2,1,0:T(8,128)(2,1)}), bf16[4,1,32,1536]{3,2,1,0:T(8,128)(2,1)S(1)}, u32[]{:S(2)}, u32[]{:S(2)}) async-start(bf16[4,1,32,1536]{3,2,1,0:T(8,128)(2,1)} %bitcast.22), calls=%async_computation.5 | async-start | bytes 786432 | tf_op jit(solution)/shard_map/all_to_all | solution.py:124
  73.2 46.6 %all-to-all-start.6 = ((bf16[4,1,32,1536]{3,2,1,0:T(8,128)(2,1)}), bf16[4,1,32,1536]{3,2,1,0:T(8,128)(2,1)S(1)}, u32[]{:S(2)}, u32[]{:S(2)}) async-start(bf16[4,1,32,1536]{3,2,1,0:T(8,128)(2,1)} %bitcast.25), calls=%async_computation.6 | async-start | bytes 786432 | tf_op jit(solution)/shard_map/all_to_all | solution.py:125
where the time goes:
time: 123 us; the launch traced here: 122 us
  blocking collectives  41.7 us (34%)
  starting transfers between devices  25.2 us (20%)
  waiting for transfers between devices  24.9 us (20%)
  local copies, waits for them, and re-layouts  16.2 us (13%)
  matrix products  8.24 us (7%)
  other arithmetic  4.98 us (4%)
    psum x1, blocking collectives, on_device(): lax.psum(jnp.stack([spatial_part, temporal_part]), ('frame', 'clip'))  41.7 us
    unnamed x29, local copies, waits for them, and re-layouts  8.53 us
    all_to_all x1, waiting for transfers between devices, on_device(): lax.all_to_all(to_groups(across_time_asker_matrix), 'frame', split_axis=1...  5.73 us
    all_to_all x1, waiting for transfers between devices, on_device(): lax.all_to_all(unrolled_vector[1], 'frame', split_axis=0, concat_axis=1,...  5.69 us
    all_to_all x1, waiting for transfers between devices, on_device(): lax.all_to_all(to_groups(across_time_payload_matrix), 'frame', split_axis...  4.97 us
    all_to_all x1, starting transfers between devices, on_device(): lax.all_to_all(to_groups(across_time_matcher_matrix), 'frame', split_axis...  4.35 us
    reshape x4, local copies, waits for them, and re-layouts, across_time_elements(): piece.reshape(frames, count, channel_bundle, features // channel_bundle)  4.32 us
    all_to_all x1, waiting for transfers between devices, on_device(): lax.all_to_all(unrolled_vector[0], 'frame', split_axis=0, concat_axis=1,...  4.3 us
  transfers between devices with their start and end apart: 7, of which 6 were waited for; matrix products, arithmetic and copies ran while one was open for 16% of the time, Pallas kernels for 0%

commit v1 on v0

v1 whole, which is shorter than its diff:
```python
import functools
import math

import jax
import jax.numpy as jnp
from jax import lax
from jax.experimental import pallas as pl
from jax.experimental.pallas import tpu as pltpu
from jax.sharding import PartitionSpec as P

F32 = jnp.float32
BF16 = jnp.bfloat16
LANES = 128
HALF = 64
CHUNKS = 4
HEADS_AT_ONCE = 4


def contract(left, right, left_dim, right_dim):
    return lax.dot_general(
        left, right, (((left_dim,), (right_dim,)), ((), ())), preferred_element_type=F32
    )


def kernel(
    frames,
    clips,
    heads,
    scale_norm,
    sharp,
    sq_in,
    sk_in,
    sv_in,
    sc_in,
    tq_in,
    tk_in,
    tv_in,
    tc_in,
    sdq,
    sdk,
    tdq,
    tdk,
    tdv,
    logit,
    sq,
    sk,
    sv,
    sc,
    tq,
    tk,
    tv,
    tc,
    far,
    raw_s,
    grad_s,
    mix_out,
    mix_in,
    logit_rows,
    logit_heads,
    sum_frame,
    sum_clip,
    load_sem,
    cross_send,
    mate_send,
    pass_send,
    mix_send,
    frame_send,
    clip_send,
    far_recv,
    mix_recv,
    frame_recv,
    clip_recv,
):
    me = lax.axis_index("frame")
    clip = lax.axis_index("clip")
    chips = frames // 2
    chip, core = me // 2, lax.rem(me, 2)
    mate = chip * 2 + 1 - core
    patches, features = sq.shape
    width = features // heads
    block = patches // CHUNKS
    inv = 1.0 / math.sqrt(width)
    others = range(1, chips)

    def rows(c):
        return pl.ds(pl.multiple_of(c * block, block), block)

    def cols(h):
        return slice(h * width, (h + 1) * width)

    def remote(src, dst, send, recv, axis, target):
        return pltpu.make_async_remote_copy(
            src_ref=src,
            dst_ref=dst,
            send_sem=send,
            recv_sem=recv,
            device_id={axis: target},
            device_id_type=pl.DeviceIdType.MESH,
        )

    def far_copy(part, slot, c, src, send, target):
        return remote(
            src.at[rows(c)], far.at[part, slot, rows(c)], send, far_recv.at[part, slot, c], "frame", target
        )

    def far_here(part, slot, c):
        remote(
            far.at[part, slot, rows(c)],
            far.at[part, slot, rows(c)],
            mate_send.at[part, c],
            far_recv.at[part, slot, c],
            "frame",
            mate,
        ).wait_recv()

    def chip_at(d):
        return lax.rem(chip + d, chips)

    loads = [
        pltpu.make_async_copy(src, dst, load_sem.at[i])
        for i, (src, dst) in enumerate(
            ((sq_in, sq), (sk_in, sk), (sv_in, sv), (sc_in, sc), (tq_in, tq), (tk_in, tk), (tv_in, tv), (tc_in, tc))
        )
    ]
    for load in loads:
        load.start()

    barrier = pltpu.get_barrier_semaphore()
    for d in range(1, frames):
        pl.semaphore_signal(
            barrier, inc=1, device_id={"frame": lax.rem(me + d, frames)}, device_id_type=pl.DeviceIdType.MESH
        )
    for d in range(1, clips):
        pl.semaphore_signal(
            barrier, inc=1, device_id={"clip": lax.rem(clip + d, clips)}, device_id_type=pl.DeviceIdType.MESH
        )
    pl.semaphore_wait(barrier, frames + clips - 2)

    def send_to(target, c, sems):
        @pl.when(target < me)
        def _():
            far_copy(0, me, c, tq_in, sems(0), target).start()
            far_copy(1, me, c, tc_in, sems(1), target).start()

        @pl.when(target > me)
        def _():
            far_copy(0, me, c, tk_in, sems(0), target).start()
            far_copy(1, me, c, tv_in, sems(1), target).start()

    for c in range(CHUNKS):
        for d in others:
            send_to(chip_at(d) * 2 + core, c, lambda part: cross_send.at[part, d, c])
        send_to(mate, c, lambda part: mate_send.at[part, c])

    logit_rows[...] = jnp.zeros_like(logit_rows)
    logit_heads[...] = jnp.zeros_like(logit_heads)
    lane_row = lax.broadcasted_iota(jnp.int32, (1, LANES), 1)
    sharp_lanes = jnp.zeros((1, LANES), F32)
    for h in range(heads):
        sharp_lanes = jnp.where(lane_row == h, sharp[1, h], sharp_lanes)
    lane = lax.broadcasted_iota(jnp.int32, (block, LANES), 1)

    for load in loads:
        load.wait()

    def spatial(h):
        at = pl.ds(pl.multiple_of(h * width, width), width)
        query, key, value, cotangent = sq[:, at], sk[:, at], sv[:, at], sc[:, at]
        sharpness = sharp[0, h]
        raw = contract(query, key, 1, 1) * inv
        scores = raw * sharpness
        exponent = jnp.exp(scores - jnp.max(scores, axis=1, keepdims=True))
        weights = exponent * (1.0 / jnp.sum(exponent, axis=1, keepdims=True))
        weight_grad = contract(cotangent, value, 1, 1)
        delta = jnp.sum(weights * weight_grad, axis=1, keepdims=True)
        score_grad = weights * (weight_grad - delta)
        low = score_grad.astype(BF16)
        factor = sharpness * inv
        sdq[:, at] = (contract(low, key, 1, 0) * factor).astype(BF16)
        sdk[:, at] = (contract(low, query, 0, 0) * factor).astype(BF16)
        logit_heads[pl.ds(h, 1), :] = jnp.sum(score_grad * raw, axis=0, keepdims=True)

    def dots(left, right):
        out = jnp.zeros((block, LANES), F32)
        for h in range(heads):
            product = left(cols(h)).astype(F32) * right(cols(h)).astype(F32)
            out = jnp.where(lane == h, jnp.sum(product, axis=1, keepdims=True), out)
        return out

    def spread(mix, at):
        return jnp.broadcast_to(mix[:, at : at + 1], (block, width))

    def row_part(c):
        r = rows(c)
        for part in range(2):
            far_here(part, mate, c)
            for d in others:
                far_here(part, chip_at(d) * 2 + 1 - core, c)
        raw_own = dots(lambda s: tq[r, s], lambda s: tk[r, s]) * inv
        grad_own = dots(lambda s: tc[r, s], lambda s: tv[r, s])

        @pl.loop(0, me)
        def _(j):
            raw_s[j] = dots(lambda s: tq[r, s], lambda s: far[0, j, r, s]) * inv
            grad_s[j] = dots(lambda s: tc[r, s], lambda s: far[1, j, r, s])

        top = lax.fori_loop(
            0, me, lambda j, top: jnp.maximum(top, raw_s[j] * sharp_lanes), raw_own * sharp_lanes
        )

        def add(j, carry):
            exponent = jnp.exp(raw_s[j] * sharp_lanes - top)
            return carry[0] + exponent, carry[1] + exponent * grad_s[j]

        exponent_own = jnp.exp(raw_own * sharp_lanes - top)
        total, mean = lax.fori_loop(0, me, add, (exponent_own, exponent_own * grad_own))
        over = 1.0 / total
        delta = mean * over

        def mixed(exponent, raw, grad):
            weights = exponent * over
            score_grad = weights * (grad - delta)
            logit_rows[...] += score_grad * raw
            return jnp.where(lane < HALF, weights, pltpu.roll(score_grad, HALF, 1)).astype(BF16)

        mix_out[me, r] = mixed(exponent_own, raw_own, grad_own)

        @pl.loop(0, me)
        def _(j):
            mix_out[j, r] = mixed(jnp.exp(raw_s[j] * sharp_lanes - top), raw_s[j], grad_s[j])
            remote(
                mix_out.at[j, r], mix_in.at[me, r], mix_send.at[j, c], mix_recv.at[me, c], "frame", j
            ).start()

        for first in range(0, heads, HEADS_AT_ONCE):
            some = range(first, min(first + HEADS_AT_ONCE, heads))

            def add_key(j, sums):
                mix = mix_out[j, r].astype(F32)
                return tuple(
                    t + spread(mix, HALF + h) * far[0, j, r, cols(h)].astype(F32) for t, h in zip(sums, some)
                )

            mix = mix_out[me, r].astype(F32)
            sums = tuple(spread(mix, HALF + h) * tk[r, cols(h)].astype(F32) for h in some)
            sums = lax.fori_loop(0, me, add_key, sums)
            for t, h in zip(sums, some):
                tdq[r, cols(h)] = (t * (sharp[1, h] * inv)).astype(BF16)

    def column_part(c):
        r = rows(c)

        @pl.loop(me + 1, frames)
        def _(i):
            remote(
                mix_out.at[me, r], mix_in.at[i, r], mix_send.at[me, c], mix_recv.at[i, c], "frame", mate
            ).wait_recv()

        for first in range(0, heads, HEADS_AT_ONCE):
            some = range(first, min(first + HEADS_AT_ONCE, heads))

            def add_row(i, sums):
                mix = mix_in[i, r].astype(F32)
                return tuple(
                    (
                        v + spread(mix, h) * far[1, i, r, cols(h)].astype(F32),
                        k + spread(mix, HALF + h) * far[0, i, r, cols(h)].astype(F32),
                    )
                    for (v, k), h in zip(sums, some)
                )

            mix = mix_out[me, r].astype(F32)
            sums = tuple(
                (
                    spread(mix, h) * tc[r, cols(h)].astype(F32),
                    spread(mix, HALF + h) * tq[r, cols(h)].astype(F32),
                )
                for h in some
            )
            sums = lax.fori_loop(me + 1, frames, add_row, sums)
            for (v, k), h in zip(sums, some):
                tdv[r, cols(h)] = v.astype(BF16)
                tdk[r, cols(h)] = (k * (sharp[1, h] * inv)).astype(BF16)

    def share(buffer, send, recv, axis, mine, size):
        for d in range(1, size):
            remote(
                buffer.at[mine], buffer.at[mine], send.at[d], recv.at[mine], axis, lax.rem(mine + d, size)
            ).start()

    def shared(buffer, send, recv, axis, mine, size):
        for d in range(1, size):
            slot = lax.rem(mine + d, size)
            remote(buffer.at[slot], buffer.at[slot], send.at[d], recv.at[slot], axis, slot).wait_recv()
        total = buffer[0]
        for i in range(1, size):
            total = total + buffer[i]
        return total

    per_step = -(-heads // CHUNKS)

    @pl.loop(0, CHUNKS)
    def _(c):
        for t in range(per_step):
            h = c * per_step + t
            if heads % CHUNKS == 0:
                spatial(h)
            else:
                pl.when(h < heads)(functools.partial(spatial, h))

        @pl.when(c >= 1)
        def _():
            row_part(c - 1)

        @pl.when(c >= 2)
        def _():
            column_part(c - 2)

        for part in range(2):
            for d in others:
                slot = chip_at(d) * 2 + core
                far_here(part, slot, c)
                far_copy(part, slot, c, far.at[part, slot], pass_send.at[part, d, c], mate).start()

    row_part(CHUNKS - 1)

    per_head = jnp.sum(logit_heads[...], axis=1, keepdims=True)
    tall = logit_heads.shape[0]
    own_lane = lax.broadcasted_iota(jnp.int32, (tall, LANES), 0) == lax.broadcasted_iota(
        jnp.int32, (tall, LANES), 1
    )
    spatial_sum = jnp.sum(jnp.where(own_lane, per_head, 0.0), axis=0, keepdims=True)
    temporal_sum = jnp.sum(logit_rows[...], axis=0, keepdims=True)
    which = lax.broadcasted_iota(jnp.int32, (8, LANES), 0)
    sum_frame[me] = jnp.where(which == 0, spatial_sum, jnp.where(which == 1, temporal_sum, 0.0))
    share(sum_frame, frame_send, frame_recv, "frame", me, frames)
    column_part(CHUNKS - 2)
    sum_clip[clip] = shared(sum_frame, frame_send, frame_recv, "frame", me, frames)
    share(sum_clip, clip_send, clip_recv, "clip", clip, clips)
    column_part(CHUNKS - 1)
    total = shared(sum_clip, clip_send, clip_recv, "clip", clip, clips)
    logit[...] = total[0:2, 0:heads] * scale_norm

    for d in range(1, frames):
        remote(sum_frame.at[me], sum_frame.at[me], frame_send.at[d], frame_recv.at[me], "frame", mate).wait_send()
    for d in range(1, clips):
        remote(sum_clip.at[clip], sum_clip.at[clip], clip_send.at[d], clip_recv.at[clip], "frame", mate).wait_send()

    @pl.loop(0, CHUNKS)
    def _(c):
        for part in range(2):
            far_copy(part, me, c, tq_in, mate_send.at[part, c], mate).wait_send()
            for d in others:
                far_copy(part, me, c, tq_in, cross_send.at[part, d, c], mate).wait_send()
                slot = chip_at(d) * 2 + core
                far_copy(part, slot, c, far.at[part, slot], pass_send.at[part, d, c], mate).wait_send()

        @pl.loop(0, me)
        def _(j):
            r = rows(c)
            remote(
                mix_out.at[j, r], mix_in.at[me, r], mix_send.at[j, c], mix_recv.at[me, c], "frame", mate
            ).wait_send()


def on_device(sq, sk, sv, sc, tq, tk, tv, tc, sharpness):
    frames, clips = lax.axis_size("frame"), lax.axis_size("clip")
    heads = sharpness.shape[1]
    full = sq.shape
    patches, features = full[2], full[3]
    block = patches // CHUNKS
    chips = frames // 2
    flat = [x.reshape(patches, features) for x in (sq, sk, sv, sc, tq, tk, tv, tc)]
    plane = jax.ShapeDtypeStruct((patches, features), BF16)
    scale_norm = 1.0 / math.sqrt(clips * full[0] * frames * full[1] * patches)
    dma = pltpu.SemaphoreType.DMA
    out = pl.pallas_call(
        functools.partial(kernel, frames, clips, heads, scale_norm),
        out_shape=(plane,) * 5 + (jax.ShapeDtypeStruct((2, heads), F32),),
        in_specs=[pl.BlockSpec(memory_space=pltpu.SMEM)] + [pl.BlockSpec(memory_space=pl.ANY)] * 8,
        out_specs=(pl.BlockSpec(memory_space=pltpu.VMEM),) * 6,
        scratch_shapes=[pltpu.VMEM((patches, features), BF16)] * 8
        + [
            pltpu.VMEM((2, frames, patches, features), BF16),
            pltpu.VMEM((frames, block, LANES), F32),
            pltpu.VMEM((frames, block, LANES), F32),
            pltpu.VMEM((frames, patches, LANES), BF16),
            pltpu.VMEM((frames, patches, LANES), BF16),
            pltpu.VMEM((block, LANES), F32),
            pltpu.VMEM((-(-heads // 8) * 8, patches), F32),
            pltpu.VMEM((frames, 8, LANES), F32),
            pltpu.VMEM((clips, 8, LANES), F32),
            dma((8,)),
            dma((2, chips, CHUNKS)),
            dma((2, CHUNKS)),
            dma((2, chips, CHUNKS)),
            dma((frames, CHUNKS)),
            dma((frames,)),
            dma((clips,)),
            dma((2, frames, CHUNKS)),
            dma((frames, CHUNKS)),
            dma((frames,)),
            dma((clips,)),
        ],
        compiler_params=pltpu.CompilerParams(
            collective_id=0, has_side_effects=True, vmem_limit_bytes=48 * 1024 * 1024
        ),
    )(sharpness, *flat)
    return tuple(x.reshape(full) for x in out[:5]) + (out[5],)


def solution(mesh):
    part = P("clip", "frame", None, None)
    return jax.shard_map(
        on_device,
        mesh=mesh,
        in_specs=(part,) * 8 + (P(),),
        out_specs=(part,) * 5 + (P(),),
        check_vma=False,
    )
```

time: 123 us -> 52.9 us (0.43)
  blocking collectives: 41.7 us -> 0 us
  Pallas kernels: 0 us -> 38.9 us
  starting transfers between devices: 25.2 us -> 0 us
  waiting for transfers between devices: 24.9 us -> 0 us
  matrix products: 8.24 us -> 0 us
  other arithmetic: 4.98 us -> 0 us
  local copies, waits for them, and re-layouts: 16.2 us -> 12.9 us
    psum x1 -> x0, blocking collectives: 41.7 us -> none  [on_device(): lax.psum(jnp.stack([spatial_part, temporal_part]), ('frame', 'clip'))]
    pallas_call x0 -> x1, Pallas kernels: none -> 38.9 us  [on_device(): pl.pallas_call(functools.partial(kernel, frames, clips, heads, scale_norm...]
    all_to_all x7 -> x0, starting transfers between devices: 25.2 us -> none  [the longest x1 4.35 us: on_device(): lax.all_to_all(to_groups(across_time_matcher_matrix), 'frame', split_axis...]
    all_to_all x7 -> x0, waiting for transfers between devices: 24.9 us -> none  [the longest x1 5.73 us: on_device(): lax.all_to_all(to_groups(across_time_asker_matrix), 'frame', split_axis=1...]
    dot_general x9 -> x0, matrix products: 8.24 us -> none  [the longest x2 3.62 us: softmax_mixing_reverse_pass(): jnp.einsum('lbhk,mbhk->bhlm', cotangent, values, preferred_element_type=j...]
    reshape x7 -> x0, local copies, waits for them, and re-layouts: 7.37 us -> none  [the longest x4 4.32 us: across_time_elements(): piece.reshape(frames, count, channel_bundle, features // channel_bundle)]
    unnamed x29 -> x24, local copies, waits for them, and re-layouts: 8.53 us -> 12.9 us
    sub x2 -> x0, other arithmetic: 2.71 us -> none  [softmax_mixing_reverse_pass(): exponent = jnp.exp(scores - row_max)]
  transfers between devices with their start and end apart: 7 -> 0, of which waited for: 6 -> 0; matrix products, arithmetic and copies ran while one was open for 16% -> 0% of each run, Pallas kernels for 0% -> 0%
where the time goes in v1:
time: 52.9 us; the launch traced here: 52.5 us
  Pallas kernels  38.9 us (74%)
  local copies, waits for them, and re-layouts  12.9 us (24%)
  between operations  0.66 us (1%)
    pallas_call x1, Pallas kernels, on_device(): pl.pallas_call(functools.partial(kernel, frames, clips, heads, scale_norm...  38.9 us
    unnamed x24, local copies, waits for them, and re-layouts  12.9 us

profile of v1, /device:TPU:0, one launch (start us, length us, event | category | flops | bytes accessed | tf_op | source)
XLA Modules:
  0.0 52.5 jit_solution(8123762007217302705)
XLA Ops:
  0.6 0.0 copy-start.8
  0.6 0.7 %copy-done.8 = f32[2,12]{1,0:T(2,128)S(1)} copy-done((f32[2,12]{1,0:T(2,128)S(1)}, f32[2,12]{1,0:T(2,128)}, u32[]{:S(2)}) %copy-start.8) | copy-done | bytes 120
  1.3 0.0 copy-start
  1.3 1.0 %copy-done = bf16[1,1,128,1536]{3,2,1,0:T(8,128)(2,1)S(1)} copy-done((bf16[1,1,128,1536]{3,2,1,0:T(8,128)(2,1)S(1)}, bf16[1,1,128,1536]{3,2,1,0:T(8,128)(2,1)}, u32[]{:S(2)}) %copy-start) | copy-done | bytes 393240
  2.3 0.0 copy-start.1
  2.3 1.0 %copy-done.1 = bf16[1,1,128,1536]{3,2,1,0:T(8,128)(2,1)S(1)} copy-done((bf16[1,1,128,1536]{3,2,1,0:T(8,128)(2,1)S(1)}, bf16[1,1,128,1536]{3,2,1,0:T(8,128)(2,1)}, u32[]{:S(2)}) %copy-start.1) | copy-done | bytes 393240
  3.3 0.0 copy-start.2
  3.3 1.0 %copy-done.2 = bf16[1,1,128,1536]{3,2,1,0:T(8,128)(2,1)S(1)} copy-done((bf16[1,1,128,1536]{3,2,1,0:T(8,128)(2,1)S(1)}, bf16[1,1,128,1536]{3,2,1,0:T(8,128)(2,1)}, u32[]{:S(2)}) %copy-start.2) | copy-done | bytes 393240
  4.3 0.0 copy-start.3
  4.3 1.0 %copy-done.3 = bf16[1,1,128,1536]{3,2,1,0:T(8,128)(2,1)S(1)} copy-done((bf16[1,1,128,1536]{3,2,1,0:T(8,128)(2,1)S(1)}, bf16[1,1,128,1536]{3,2,1,0:T(8,128)(2,1)}, u32[]{:S(2)}) %copy-start.3) | copy-done | bytes 393240
  5.3 0.0 copy-start.4
  5.3 1.0 %copy-done.4 = bf16[1,1,128,1536]{3,2,1,0:T(8,128)(2,1)S(1)} copy-done((bf16[1,1,128,1536]{3,2,1,0:T(8,128)(2,1)S(1)}, bf16[1,1,128,1536]{3,2,1,0:T(8,128)(2,1)}, u32[]{:S(2)}) %copy-start.4) | copy-done | bytes 393240
  6.3 0.0 copy-start.5
  6.3 1.0 %copy-done.5 = bf16[1,1,128,1536]{3,2,1,0:T(8,128)(2,1)S(1)} copy-done((bf16[1,1,128,1536]{3,2,1,0:T(8,128)(2,1)S(1)}, bf16[1,1,128,1536]{3,2,1,0:T(8,128)(2,1)}, u32[]{:S(2)}) %copy-start.5) | copy-done | bytes 393240
  7.3 0.0 copy-start.6
  7.3 1.0 %copy-done.6 = bf16[1,1,128,1536]{3,2,1,0:T(8,128)(2,1)S(1)} copy-done((bf16[1,1,128,1536]{3,2,1,0:T(8,128)(2,1)S(1)}, bf16[1,1,128,1536]{3,2,1,0:T(8,128)(2,1)}, u32[]{:S(2)}) %copy-start.6) | copy-done | bytes 393240
  8.3 0.0 copy-start.7
  8.3 1.0 %copy-done.7 = bf16[1,1,128,1536]{3,2,1,0:T(8,128)(2,1)S(1)} copy-done((bf16[1,1,128,1536]{3,2,1,0:T(8,128)(2,1)S(1)}, bf16[1,1,128,1536]{3,2,1,0:T(8,128)(2,1)}, u32[]{:S(2)}) %copy-start.7) | copy-done | bytes 393240
  9.3 38.9 %shard_map.136 = (bf16[128,1536]{1,0:T(8,128)(2,1)S(1)}, bf16[128,1536]{1,0:T(8,128)(2,1)S(1)}, bf16[128,1536]{1,0:T(8,128)(2,1)S(1)}, bf16[128,1536]{1,0:T(8,12...) custom-call(f32[2,12]{1,0:T(2,128)S(1)} %copy-done.8, bf16[128,1536]{1,0:T(8,128)(2,1)S(1)} %bitcast.18, ...), custom_call_target="tpu_custom_call" | custom-call | tf_op jit(solution)/shard_map/pallas_call | solution.py:377
  48.2 0.7 %copy.21 = bf16[1,1,128,1536]{3,2,1,0:T(8,128)(2,1)} copy(bf16[1,1,128,1536]{3,2,1,0:T(8,128)(2,1)S(1)} %bitcast.17) | data formatting | bytes 786432
  48.9 0.7 %copy.22 = bf16[1,1,128,1536]{3,2,1,0:T(8,128)(2,1)} copy(bf16[1,1,128,1536]{3,2,1,0:T(8,128)(2,1)S(1)} %bitcast.16) | data formatting | bytes 786432
  49.7 0.7 %copy.23 = bf16[1,1,128,1536]{3,2,1,0:T(8,128)(2,1)} copy(bf16[1,1,128,1536]{3,2,1,0:T(8,128)(2,1)S(1)} %bitcast.15) | data formatting | bytes 786432
  50.4 0.7 %copy.24 = bf16[1,1,128,1536]{3,2,1,0:T(8,128)(2,1)} copy(bf16[1,1,128,1536]{3,2,1,0:T(8,128)(2,1)S(1)} %bitcast.14) | data formatting | bytes 786432
  51.2 0.7 %copy.25 = bf16[1,1,128,1536]{3,2,1,0:T(8,128)(2,1)} copy(bf16[1,1,128,1536]{3,2,1,0:T(8,128)(2,1)S(1)} %bitcast.13) | data formatting | bytes 786432
  51.9 0.6 %copy.26 = f32[2,12]{1,0:T(2,128)} copy(f32[2,12]{1,0:T(2,128)S(1)} %get-tuple-element.29) | data formatting | bytes 192
Async XLA Ops:
  0.6 0.7 %copy-start.8 = (f32[2,12]{1,0:T(2,128)S(1)}, f32[2,12]{1,0:T(2,128)}, u32[]{:S(2)}) copy-start(f32[2,12]{1,0:T(2,128)} %sharp.1) | copy-start | bytes 292
  1.3 1.0 %copy-start = (bf16[1,1,128,1536]{3,2,1,0:T(8,128)(2,1)S(1)}, bf16[1,1,128,1536]{3,2,1,0:T(8,128)(2,1)}, u32[]{:S(2)}) copy-start(bf16[1,1,128,1536]{3,2,1,0:T(8,128)(2,1)} %param.9) | copy-start | bytes 1179652
  2.3 1.0 %copy-start.1 = (bf16[1,1,128,1536]{3,2,1,0:T(8,128)(2,1)S(1)}, bf16[1,1,128,1536]{3,2,1,0:T(8,128)(2,1)}, u32[]{:S(2)}) copy-start(bf16[1,1,128,1536]{3,2,1,0:T(8,128)(2,1)} %param.10) | copy-start | bytes 1179652
  3.3 1.0 %copy-start.2 = (bf16[1,1,128,1536]{3,2,1,0:T(8,128)(2,1)S(1)}, bf16[1,1,128,1536]{3,2,1,0:T(8,128)(2,1)}, u32[]{:S(2)}) copy-start(bf16[1,1,128,1536]{3,2,1,0:T(8,128)(2,1)} %param.11) | copy-start | bytes 1179652
  4.3 1.0 %copy-start.3 = (bf16[1,1,128,1536]{3,2,1,0:T(8,128)(2,1)S(1)}, bf16[1,1,128,1536]{3,2,1,0:T(8,128)(2,1)}, u32[]{:S(2)}) copy-start(bf16[1,1,128,1536]{3,2,1,0:T(8,128)(2,1)} %param.12) | copy-start | bytes 1179652
  5.3 1.0 %copy-start.4 = (bf16[1,1,128,1536]{3,2,1,0:T(8,128)(2,1)S(1)}, bf16[1,1,128,1536]{3,2,1,0:T(8,128)(2,1)}, u32[]{:S(2)}) copy-start(bf16[1,1,128,1536]{3,2,1,0:T(8,128)(2,1)} %param.13) | copy-start | bytes 1179652
  6.3 1.0 %copy-start.5 = (bf16[1,1,128,1536]{3,2,1,0:T(8,128)(2,1)S(1)}, bf16[1,1,128,1536]{3,2,1,0:T(8,128)(2,1)}, u32[]{:S(2)}) copy-start(bf16[1,1,128,1536]{3,2,1,0:T(8,128)(2,1)} %param.14) | copy-start | bytes 1179652
  7.3 1.0 %copy-start.6 = (bf16[1,1,128,1536]{3,2,1,0:T(8,128)(2,1)S(1)}, bf16[1,1,128,1536]{3,2,1,0:T(8,128)(2,1)}, u32[]{:S(2)}) copy-start(bf16[1,1,128,1536]{3,2,1,0:T(8,128)(2,1)} %param.15) | copy-start | bytes 1179652
  8.3 1.0 %copy-start.7 = (bf16[1,1,128,1536]{3,2,1,0:T(8,128)(2,1)S(1)}, bf16[1,1,128,1536]{3,2,1,0:T(8,128)(2,1)}, u32[]{:S(2)}) copy-start(bf16[1,1,128,1536]{3,2,1,0:T(8,128)(2,1)} %param.16) | copy-start | bytes 1179652

commit v2 on v1

--- a/solution.py
+++ b/solution.py
@@ -13,7 +13,9 @@
 LANES = 128
 HALF = 64
 CHUNKS = 4
-HEADS_AT_ONCE = 4
+SPLIT = 2
+AHEAD = 3
+HEADS_AT_ONCE = 6
 
 
 def contract(left, right, left_dim, right_dim):
@@ -27,7 +29,7 @@
     clips,
     heads,
     scale_norm,
-    sharp,
+    sharp_in,
     sq_in,
     sk_in,
     sv_in,
@@ -42,6 +44,7 @@
     tdk,
     tdv,
     logit,
+    sharp,
     sq,
     sk,
     sv,
@@ -79,6 +82,8 @@
     patches, features = sq.shape
     width = features // heads
     block = patches // CHUNKS
+    pieces = CHUNKS * SPLIT
+    piece = block // SPLIT
     inv = 1.0 / math.sqrt(width)
     others = range(1, chips)
 
@@ -98,20 +103,14 @@
             device_id_type=pl.DeviceIdType.MESH,
         )
 
-    def far_copy(part, slot, c, src, send, target):
-        return remote(
-            src.at[rows(c)], far.at[part, slot, rows(c)], send, far_recv.at[part, slot, c], "frame", target
-        )
-
-    def far_here(part, slot, c):
-        remote(
-            far.at[part, slot, rows(c)],
-            far.at[part, slot, rows(c)],
-            mate_send.at[part, c],
-            far_recv.at[part, slot, c],
-            "frame",
-            mate,
-        ).wait_recv()
+    def piece_rows(p):
+        return pl.ds(pl.multiple_of(p * piece, piece), piece)
+
+    def far_copy(part, slot, r, at, src, send, target):
+        return remote(src.at[r], far.at[part, slot, r], send, far_recv.at[part, slot, at], "frame", target)
+
+    def far_here(part, slot, r, at):
+        far_copy(part, slot, r, at, far.at[part, slot], mate_send.at[part, 0], mate).wait_recv()
 
     def chip_at(d):
         return lax.rem(chip + d, chips)
@@ -119,7 +118,7 @@
     loads = [
         pltpu.make_async_copy(src, dst, load_sem.at[i])
         for i, (src, dst) in enumerate(
-            ((sq_in, sq), (sk_in, sk), (sv_in, sv), (sc_in, sc), (tq_in, tq), (tk_in, tk), (tv_in, tv), (tc_in, tc))
+            ((sharp_in, sharp), (sq_in, sq), (sk_in, sk), (sv_in, sv), (sc_in, sc), (tq_in, tq), (tk_in, tk), (tv_in, tv), (tc_in, tc))
         )
     ]
     for load in loads:
@@ -136,32 +135,39 @@
         )
     pl.semaphore_wait(barrier, frames + clips - 2)
 
-    def send_to(target, c, sems):
+    def send_to(target, r, at, sems):
         @pl.when(target < me)
         def _():
-            far_copy(0, me, c, tq_in, sems(0), target).start()
-            far_copy(1, me, c, tc_in, sems(1), target).start()
+            far_copy(0, me, r, at, tq_in, sems(0), target).start()
+            far_copy(1, me, r, at, tc_in, sems(1), target).start()
 
         @pl.when(target > me)
         def _():
-            far_copy(0, me, c, tk_in, sems(0), target).start()
-            far_copy(1, me, c, tv_in, sems(1), target).start()
-
+            far_copy(0, me, r, at, tk_in, sems(0), target).start()
+            far_copy(1, me, r, at, tv_in, sems(1), target).start()
+
+    def send_far(p):
+        for d in others:
+            send_to(chip_at(d) * 2 + core, piece_rows(p), p, lambda part: cross_send.at[part, d, p])
+
+    for p in range(AHEAD):
+        send_far(p)
     for c in range(CHUNKS):
-        for d in others:
-            send_to(chip_at(d) * 2 + core, c, lambda part: cross_send.at[part, d, c])
-        send_to(mate, c, lambda part: mate_send.at[part, c])
-
+        send_to(mate, rows(c), c, lambda part: mate_send.at[part, c])
+
+    raw_s[...] = jnp.zeros_like(raw_s)
+    grad_s[...] = jnp.zeros_like(grad_s)
     logit_rows[...] = jnp.zeros_like(logit_rows)
     logit_heads[...] = jnp.zeros_like(logit_heads)
+    for load in loads:
+        load.wait()
+
     lane_row = lax.broadcasted_iota(jnp.int32, (1, LANES), 1)
     sharp_lanes = jnp.zeros((1, LANES), F32)
     for h in range(heads):
         sharp_lanes = jnp.where(lane_row == h, sharp[1, h], sharp_lanes)
     lane = lax.broadcasted_iota(jnp.int32, (block, LANES), 1)
-
-    for load in loads:
-        load.wait()
+    place = jnp.full((block, LANES), me, jnp.int32)
 
     def spatial(h):
         at = pl.ds(pl.multiple_of(h * width, width), width)
@@ -193,9 +199,10 @@
     def row_part(c):
         r = rows(c)
         for part in range(2):
-            far_here(part, mate, c)
+            far_here(part, mate, r, c)
             for d in others:
-                far_here(part, chip_at(d) * 2 + 1 - core, c)
+                for p in range(SPLIT):
+                    far_here(part, chip_at(d) * 2 + 1 - core, piece_rows(c * SPLIT + p), c * SPLIT + p)
         raw_own = dots(lambda s: tq[r, s], lambda s: tk[r, s]) * inv
         grad_own = dots(lambda s: tc[r, s], lambda s: tv[r, s])
 
@@ -204,33 +211,43 @@
             raw_s[j] = dots(lambda s: tq[r, s], lambda s: far[0, j, r, s]) * inv
             grad_s[j] = dots(lambda s: tc[r, s], lambda s: far[1, j, r, s])
 
-        top = lax.fori_loop(
-            0, me, lambda j, top: jnp.maximum(top, raw_s[j] * sharp_lanes), raw_own * sharp_lanes
-        )
-
-        def add(j, carry):
-            exponent = jnp.exp(raw_s[j] * sharp_lanes - top)
-            return carry[0] + exponent, carry[1] + exponent * grad_s[j]
-
-        exponent_own = jnp.exp(raw_own * sharp_lanes - top)
-        total, mean = lax.fori_loop(0, me, add, (exponent_own, exponent_own * grad_own))
+        scores_own = raw_own * sharp_lanes
+        raw = [raw_s[j] for j in range(frames - 1)]
+        grad = [grad_s[j] for j in range(frames - 1)]
+        scores = [x * sharp_lanes for x in raw]
+        top = scores_own
+        for j, x in enumerate(scores):
+            top = jnp.maximum(top, jnp.where(place > j, x, scores_own))
+        exponent_own = jnp.exp(scores_own - top)
+        exponent = [jnp.where(place > j, jnp.exp(x - top), 0.0) for j, x in enumerate(scores)]
+        total, mean = exponent_own, exponent_own * grad_own
+        for e, g in zip(exponent, grad):
+            total, mean = total + e, mean + e * g
         over = 1.0 / total
         delta = mean * over
 
-        def mixed(exponent, raw, grad):
-            weights = exponent * over
-            score_grad = weights * (grad - delta)
-            logit_rows[...] += score_grad * raw
-            return jnp.where(lane < HALF, weights, pltpu.roll(score_grad, HALF, 1)).astype(BF16)
-
-        mix_out[me, r] = mixed(exponent_own, raw_own, grad_own)
-
-        @pl.loop(0, me)
-        def _(j):
-            mix_out[j, r] = mixed(jnp.exp(raw_s[j] * sharp_lanes - top), raw_s[j], grad_s[j])
-            remote(
-                mix_out.at[j, r], mix_in.at[me, r], mix_send.at[j, c], mix_recv.at[me, c], "frame", j
-            ).start()
+        def mixed(e, g):
+            weights = e * over
+            score_grad = weights * (g - delta)
+            return score_grad, jnp.where(lane < HALF, weights, pltpu.roll(score_grad, HALF, 1)).astype(BF16)
+
+        score_grad, mix = mixed(exponent_own, grad_own)
+        mix_out[me, r] = mix
+        share_sum = score_grad * raw_own
+
+        for j in range(frames - 1):
+            score_grad, mix = mixed(exponent[j], grad[j])
+            share_sum = share_sum + score_grad * raw[j]
+
+            def send_mix(j=j, mix=mix):
+                mix_out[j, r] = mix
+                remote(
+                    mix_out.at[j, r], mix_in.at[me, r], mix_send.at[j, c], mix_recv.at[me, c], "frame", j
+                ).start()
+
+            pl.when(j < me)(send_mix)
+
+        logit_rows[...] += share_sum
 
         for first in range(0, heads, HEADS_AT_ONCE):
             some = range(first, min(first + HEADS_AT_ONCE, heads))
@@ -297,6 +314,19 @@
             total = total + buffer[i]
         return total
 
+    def take(p):
+        for part in range(2):
+            for d in others:
+                slot = chip_at(d) * 2 + core
+                far_here(part, slot, piece_rows(p), p)
+                far_copy(
+                    part, slot, piece_rows(p), p, far.at[part, slot], pass_send.at[part, d, p], mate
+                ).start()
+
+        @pl.when(p + AHEAD < pieces)
+        def _():
+            send_far(p + AHEAD)
+
     per_step = -(-heads // CHUNKS)
 
     @pl.loop(0, CHUNKS)
@@ -308,6 +338,8 @@
             else:
                 pl.when(h < heads)(functools.partial(spatial, h))
 
+        take(c * SPLIT)
+
         @pl.when(c >= 1)
         def _():
             row_part(c - 1)
@@ -316,11 +348,7 @@
         def _():
             column_part(c - 2)
 
-        for part in range(2):
-            for d in others:
-                slot = chip_at(d) * 2 + core
-                far_here(part, slot, c)
-                far_copy(part, slot, c, far.at[part, slot], pass_send.at[part, d, c], mate).start()
+        take(c * SPLIT + 1)
 
     row_part(CHUNKS - 1)
 
@@ -349,11 +377,7 @@
     @pl.loop(0, CHUNKS)
     def _(c):
         for part in range(2):
-            far_copy(part, me, c, tq_in, mate_send.at[part, c], mate).wait_send()
-            for d in others:
-                far_copy(part, me, c, tq_in, cross_send.at[part, d, c], mate).wait_send()
-                slot = chip_at(d) * 2 + core
-                far_copy(part, slot, c, far.at[part, slot], pass_send.at[part, d, c], mate).wait_send()
+            far_copy(part, me, rows(c), c, tq_in, mate_send.at[part, c], mate).wait_send()
 
         @pl.loop(0, me)
         def _(j):
@@ -361,6 +385,26 @@
             remote(
                 mix_out.at[j, r], mix_in.at[me, r], mix_send.at[j, c], mix_recv.at[me, c], "frame", mate
             ).wait_send()
+
+
+    @pl.loop(0, pieces)
+    def _(p):
+        for part in range(2):
+            for d in others:
+                slot, r = chip_at(d) * 2 + core, piece_rows(p)
+                far_copy(part, me, r, p, tq_in, cross_send.at[part, d, p], mate).wait_send()
+                far_copy(part, slot, r, p, far.at[part, slot], pass_send.at[part, d, p], mate).wait_send()
+
+
+def store_kernel(*refs):
+    count = len(refs) // 2
+    copies = [
+        pltpu.make_async_copy(refs[i], refs[count + i], refs[-1].at[i]) for i in range(count)
+    ]
+    for copy in copies:
+        copy.start()
+    for copy in copies:
+        copy.wait()
 
 
 def on_device(sq, sk, sv, sc, tq, tk, tv, tc, sharpness):
@@ -377,9 +421,10 @@
     out = pl.pallas_call(
         functools.partial(kernel, frames, clips, heads, scale_norm),
         out_shape=(plane,) * 5 + (jax.ShapeDtypeStruct((2, heads), F32),),
-        in_specs=[pl.BlockSpec(memory_space=pltpu.SMEM)] + [pl.BlockSpec(memory_space=pl.ANY)] * 8,
+        in_specs=[pl.BlockSpec(memory_space=pltpu.HBM)] * 9,
         out_specs=(pl.BlockSpec(memory_space=pltpu.VMEM),) * 6,
-        scratch_shapes=[pltpu.VMEM((patches, features), BF16)] * 8
+        scratch_shapes=[pltpu.SMEM((2, heads), F32)]
+        + [pltpu.VMEM((patches, features), BF16)] * 8
         + [
             pltpu.VMEM((2, frames, patches, features), BF16),
             pltpu.VMEM((frames, block, LANES), F32),
@@ -390,22 +435,29 @@
             pltpu.VMEM((-(-heads // 8) * 8, patches), F32),
             pltpu.VMEM((frames, 8, LANES), F32),
             pltpu.VMEM((clips, 8, LANES), F32),
-            dma((8,)),
-            dma((2, chips, CHUNKS)),
+            dma((9,)),
+            dma((2, chips, CHUNKS * SPLIT)),
             dma((2, CHUNKS)),
-            dma((2, chips, CHUNKS)),
+            dma((2, chips, CHUNKS * SPLIT)),
             dma((frames, CHUNKS)),
             dma((frames,)),
             dma((clips,)),
-            dma((2, frames, CHUNKS)),
+            dma((2, frames, CHUNKS * SPLIT)),
             dma((frames, CHUNKS)),
             dma((frames,)),
             dma((clips,)),
         ],
         compiler_params=pltpu.CompilerParams(
-            collective_id=0, has_side_effects=True, vmem_limit_bytes=48 * 1024 * 1024
+            collective_id=0, has_side_effects=True, vmem_limit_bytes=32 * 1024 * 1024
         ),
     )(sharpness, *flat)
+    out = pl.pallas_call(
+        store_kernel,
+        out_shape=(plane,) * 5 + (jax.ShapeDtypeStruct((2, heads), F32),),
+        in_specs=[pl.BlockSpec(memory_space=pltpu.VMEM)] * 6,
+        out_specs=(pl.BlockSpec(memory_space=pltpu.HBM),) * 6,
+        scratch_shapes=[dma((6,))],
+    )(*out)
     return tuple(x.reshape(full) for x in out[:5]) + (out[5],)
 
 

time: 52.9 us -> 53.5 us (1.011)
    pallas_call x0 -> x1, Pallas kernels: none -> 2.79 us  [on_device(): pl.pallas_call(store_kernel, out_shape=(plane,) * 5 + (jax.ShapeDtypeStru...]
    pallas_call x1, Pallas kernels: 38.9 us -> 36.6 us  [on_device(): pl.pallas_call(functools.partial(kernel, frames, clips, heads, scale_norm...]
    unnamed x24 -> x30, local copies, waits for them, and re-layouts: 12.9 us -> 13 us
where the time goes in v2:
time: 53.5 us; the launch traced here: 53 us
  Pallas kernels  39.4 us (74%)
  local copies, waits for them, and re-layouts  13 us (24%)
  between operations  0.67 us (1%)
    pallas_call x1, Pallas kernels, on_device(): pl.pallas_call(functools.partial(kernel, frames, clips, heads, scale_norm...  36.6 us
    unnamed x30, local copies, waits for them, and re-layouts  13 us
    pallas_call x1, Pallas kernels, on_device(): pl.pallas_call(store_kernel, out_shape=(plane,) * 5 + (jax.ShapeDtypeStru...  2.79 us

profile of v2, /device:TPU:0, one launch (start us, length us, event | category | flops | bytes accessed | tf_op | source)
XLA Modules:
  0.0 53.0 jit_solution(8744325761145435671)
XLA Ops:
  0.6 0.0 copy-start.14
  0.6 0.7 %copy-done.14 = f32[2,12]{1,0:T(2,128)S(1)} copy-done((f32[2,12]{1,0:T(2,128)S(1)}, f32[2,12]{1,0:T(2,128)}, u32[]{:S(2)}) %copy-start.14) | copy-done | bytes 120
  1.3 0.0 copy-start.5
  1.3 1.0 %copy-done.5 = bf16[1,1,128,1536]{3,2,1,0:T(8,128)(2,1)S(1)} copy-done((bf16[1,1,128,1536]{3,2,1,0:T(8,128)(2,1)S(1)}, bf16[1,1,128,1536]{3,2,1,0:T(8,128)(2,1)}, u32[]{:S(2)}) %copy-start.5) | copy-done | bytes 393240
  2.3 0.0 copy-start.6
  2.3 1.0 %copy-done.6 = bf16[1,1,128,1536]{3,2,1,0:T(8,128)(2,1)S(1)} copy-done((bf16[1,1,128,1536]{3,2,1,0:T(8,128)(2,1)S(1)}, bf16[1,1,128,1536]{3,2,1,0:T(8,128)(2,1)}, u32[]{:S(2)}) %copy-start.6) | copy-done | bytes 393240
  3.3 0.0 copy-start.7
  3.3 1.0 %copy-done.7 = bf16[1,1,128,1536]{3,2,1,0:T(8,128)(2,1)S(1)} copy-done((bf16[1,1,128,1536]{3,2,1,0:T(8,128)(2,1)S(1)}, bf16[1,1,128,1536]{3,2,1,0:T(8,128)(2,1)}, u32[]{:S(2)}) %copy-start.7) | copy-done | bytes 393240
  4.3 0.0 copy-start.8
  4.3 1.0 %copy-done.8 = bf16[1,1,128,1536]{3,2,1,0:T(8,128)(2,1)S(1)} copy-done((bf16[1,1,128,1536]{3,2,1,0:T(8,128)(2,1)S(1)}, bf16[1,1,128,1536]{3,2,1,0:T(8,128)(2,1)}, u32[]{:S(2)}) %copy-start.8) | copy-done | bytes 393240
  5.3 0.0 copy-start.9
  5.3 1.0 %copy-done.9 = bf16[1,1,128,1536]{3,2,1,0:T(8,128)(2,1)S(1)} copy-done((bf16[1,1,128,1536]{3,2,1,0:T(8,128)(2,1)S(1)}, bf16[1,1,128,1536]{3,2,1,0:T(8,128)(2,1)}, u32[]{:S(2)}) %copy-start.9) | copy-done | bytes 393240
  6.3 0.0 copy-start.10
  6.3 1.0 %copy-done.10 = bf16[1,1,128,1536]{3,2,1,0:T(8,128)(2,1)S(1)} copy-done((bf16[1,1,128,1536]{3,2,1,0:T(8,128)(2,1)S(1)}, bf16[1,1,128,1536]{3,2,1,0:T(8,128)(2,1)}, u32[]{:S(2)}) %copy-start.10) | copy-done | bytes 393240
  7.3 0.0 copy-start.11
  7.3 1.0 %copy-done.11 = bf16[1,1,128,1536]{3,2,1,0:T(8,128)(2,1)S(1)} copy-done((bf16[1,1,128,1536]{3,2,1,0:T(8,128)(2,1)S(1)}, bf16[1,1,128,1536]{3,2,1,0:T(8,128)(2,1)}, u32[]{:S(2)}) %copy-start.11) | copy-done | bytes 393240
  8.3 0.0 copy-start.12
  8.3 1.0 %copy-done.12 = bf16[1,1,128,1536]{3,2,1,0:T(8,128)(2,1)S(1)} copy-done((bf16[1,1,128,1536]{3,2,1,0:T(8,128)(2,1)S(1)}, bf16[1,1,128,1536]{3,2,1,0:T(8,128)(2,1)}, u32[]{:S(2)}) %copy-start.12) | copy-done | bytes 393240
  9.3 36.6 %shard_map.136 = (bf16[128,1536]{1,0:T(8,128)(2,1)S(1)}, bf16[128,1536]{1,0:T(8,128)(2,1)S(1)}, bf16[128,1536]{1,0:T(8,128)(2,1)S(1)}, bf16[128,1536]{1,0:T(8,12...) custom-call(f32[2,12]{1,0:T(2,128)S(1)} %copy-done.14, bf16[128,1536]{1,0:T(8,128)(2,1)S(1)} %bitcast.13, ...), custom_call_target="tpu_custom_call" | custom-call | tf_op jit(solution)/shard_map/pallas_call | solution.py:421
  45.9 0.0 copy-start
  45.9 0.7 %copy-done = bf16[128,1536]{1,0:T(8,128)(2,1)} copy-done((bf16[128,1536]{1,0:T(8,128)(2,1)}, bf16[128,1536]{1,0:T(8,128)(2,1)S(1)}, u32[]{:S(2)}) %copy-start) | copy-done | bytes 393240
  46.7 0.0 copy-start.1
  46.7 0.7 %copy-done.1 = bf16[128,1536]{1,0:T(8,128)(2,1)} copy-done((bf16[128,1536]{1,0:T(8,128)(2,1)}, bf16[128,1536]{1,0:T(8,128)(2,1)S(1)}, u32[]{:S(2)}) %copy-start.1) | copy-done | bytes 393240
  47.4 0.0 copy-start.2
  47.4 0.8 %copy-done.2 = bf16[128,1536]{1,0:T(8,128)(2,1)} copy-done((bf16[128,1536]{1,0:T(8,128)(2,1)}, bf16[128,1536]{1,0:T(8,128)(2,1)S(1)}, u32[]{:S(2)}) %copy-start.2) | copy-done | bytes 393240
  48.2 0.0 copy-start.3
  48.2 0.8 %copy-done.3 = bf16[128,1536]{1,0:T(8,128)(2,1)} copy-done((bf16[128,1536]{1,0:T(8,128)(2,1)}, bf16[128,1536]{1,0:T(8,128)(2,1)S(1)}, u32[]{:S(2)}) %copy-start.3) | copy-done | bytes 393240
  48.9 0.0 copy-start.4
  48.9 0.7 %copy-done.4 = bf16[128,1536]{1,0:T(8,128)(2,1)} copy-done((bf16[128,1536]{1,0:T(8,128)(2,1)}, bf16[128,1536]{1,0:T(8,128)(2,1)S(1)}, u32[]{:S(2)}) %copy-start.4) | copy-done | bytes 393240
  49.7 0.0 copy-start.13
  49.7 0.6 %copy-done.13 = f32[2,12]{1,0:T(2,128)} copy-done((f32[2,12]{1,0:T(2,128)}, f32[2,12]{1,0:T(2,128)S(1)}, u32[]{:S(2)}) %copy-start.13) | copy-done | bytes 120
  50.3 2.8 %shard_map.137 = (bf16[128,1536]{1,0:T(8,128)(2,1)}, bf16[128,1536]{1,0:T(8,128)(2,1)}, bf16[128,1536]{1,0:T(8,128)(2,1)}, bf16[128,1536]{1,0:T(8,128)(2,1)}, bf...) custom-call(bf16[128,1536]{1,0:T(8,128)(2,1)} %copy-done, bf16[128,1536]{1,0:T(8,128)(2,1)} %copy-done.1, ...), custom_call_target="tpu_custom_call" | custom-call | tf_op jit(solution)/shard_map/pallas_call | solution.py:454
Async XLA Ops:
  0.6 0.7 %copy-start.14 = (f32[2,12]{1,0:T(2,128)S(1)}, f32[2,12]{1,0:T(2,128)}, u32[]{:S(2)}) copy-start(f32[2,12]{1,0:T(2,128)} %sharp_in.1) | copy-start | bytes 292
  1.3 1.0 %copy-start.5 = (bf16[1,1,128,1536]{3,2,1,0:T(8,128)(2,1)S(1)}, bf16[1,1,128,1536]{3,2,1,0:T(8,128)(2,1)}, u32[]{:S(2)}) copy-start(bf16[1,1,128,1536]{3,2,1,0:T(8,128)(2,1)} %param.9) | copy-start | bytes 1179652
  2.3 1.0 %copy-start.6 = (bf16[1,1,128,1536]{3,2,1,0:T(8,128)(2,1)S(1)}, bf16[1,1,128,1536]{3,2,1,0:T(8,128)(2,1)}, u32[]{:S(2)}) copy-start(bf16[1,1,128,1536]{3,2,1,0:T(8,128)(2,1)} %param.10) | copy-start | bytes 1179652
  3.3 1.0 %copy-start.7 = (bf16[1,1,128,1536]{3,2,1,0:T(8,128)(2,1)S(1)}, bf16[1,1,128,1536]{3,2,1,0:T(8,128)(2,1)}, u32[]{:S(2)}) copy-start(bf16[1,1,128,1536]{3,2,1,0:T(8,128)(2,1)} %param.11) | copy-start | bytes 1179652
  4.3 1.0 %copy-start.8 = (bf16[1,1,128,1536]{3,2,1,0:T(8,128)(2,1)S(1)}, bf16[1,1,128,1536]{3,2,1,0:T(8,128)(2,1)}, u32[]{:S(2)}) copy-start(bf16[1,1,128,1536]{3,2,1,0:T(8,128)(2,1)} %param.12) | copy-start | bytes 1179652
  5.3 1.0 %copy-start.9 = (bf16[1,1,128,1536]{3,2,1,0:T(8,128)(2,1)S(1)}, bf16[1,1,128,1536]{3,2,1,0:T(8,128)(2,1)}, u32[]{:S(2)}) copy-start(bf16[1,1,128,1536]{3,2,1,0:T(8,128)(2,1)} %param.13) | copy-start | bytes 1179652
  6.3 1.0 %copy-start.10 = (bf16[1,1,128,1536]{3,2,1,0:T(8,128)(2,1)S(1)}, bf16[1,1,128,1536]{3,2,1,0:T(8,128)(2,1)}, u32[]{:S(2)}) copy-start(bf16[1,1,128,1536]{3,2,1,0:T(8,128)(2,1)} %param.14) | copy-start | bytes 1179652
  7.3 1.0 %copy-start.11 = (bf16[1,1,128,1536]{3,2,1,0:T(8,128)(2,1)S(1)}, bf16[1,1,128,1536]{3,2,1,0:T(8,128)(2,1)}, u32[]{:S(2)}) copy-start(bf16[1,1,128,1536]{3,2,1,0:T(8,128)(2,1)} %param.15) | copy-start | bytes 1179652
  8.3 1.0 %copy-start.12 = (bf16[1,1,128,1536]{3,2,1,0:T(8,128)(2,1)S(1)}, bf16[1,1,128,1536]{3,2,1,0:T(8,128)(2,1)}, u32[]{:S(2)}) copy-start(bf16[1,1,128,1536]{3,2,1,0:T(8,128)(2,1)} %param.16) | copy-start | bytes 1179652
  45.9 0.8 %copy-start = (bf16[128,1536]{1,0:T(8,128)(2,1)}, bf16[128,1536]{1,0:T(8,128)(2,1)S(1)}, u32[]{:S(2)}) copy-start(bf16[128,1536]{1,0:T(8,128)(2,1)S(1)} %get-tuple-element.18.refs_0_) | copy-start | bytes 1179652
  46.7 0.8 %copy-start.1 = (bf16[128,1536]{1,0:T(8,128)(2,1)}, bf16[128,1536]{1,0:T(8,128)(2,1)S(1)}, u32[]{:S(2)}) copy-start(bf16[128,1536]{1,0:T(8,128)(2,1)S(1)} %get-tuple-element.19.refs_1_) | copy-start | bytes 1179652
  47.4 0.8 %copy-start.2 = (bf16[128,1536]{1,0:T(8,128)(2,1)}, bf16[128,1536]{1,0:T(8,128)(2,1)S(1)}, u32[]{:S(2)}) copy-start(bf16[128,1536]{1,0:T(8,128)(2,1)S(1)} %get-tuple-element.20.refs_2_) | copy-start | bytes 1179652
  48.2 0.8 %copy-start.3 = (bf16[128,1536]{1,0:T(8,128)(2,1)}, bf16[128,1536]{1,0:T(8,128)(2,1)S(1)}, u32[]{:S(2)}) copy-start(bf16[128,1536]{1,0:T(8,128)(2,1)S(1)} %get-tuple-element.21.refs_3_) | copy-start | bytes 1179652
  48.9 0.8 %copy-start.4 = (bf16[128,1536]{1,0:T(8,128)(2,1)}, bf16[128,1536]{1,0:T(8,128)(2,1)S(1)}, u32[]{:S(2)}) copy-start(bf16[128,1536]{1,0:T(8,128)(2,1)S(1)} %get-tuple-element.22.refs_4_) | copy-start | bytes 1179652
  49.7 0.6 %copy-start.13 = (f32[2,12]{1,0:T(2,128)}, f32[2,12]{1,0:T(2,128)S(1)}, u32[]{:S(2)}) copy-start(f32[2,12]{1,0:T(2,128)S(1)} %get-tuple-element.23.refs_5_) | copy-start | bytes 292

commit v3 on v2

--- a/solution.py
+++ b/solution.py
@@ -16,6 +16,9 @@
 SPLIT = 2
 AHEAD = 3
 HEADS_AT_ONCE = 6
+WRITTEN_OUT = 4
+OUTPUTS = 5
+GRANT = 61 * 1024 * 1024
 
 
 def contract(left, right, left_dim, right_dim):
@@ -38,11 +41,11 @@
     tk_in,
     tv_in,
     tc_in,
-    sdq,
-    sdk,
-    tdq,
-    tdk,
-    tdv,
+    sdq_out,
+    sdk_out,
+    tdq_out,
+    tdk_out,
+    tdv_out,
     logit,
     sharp,
     sq,
@@ -53,6 +56,11 @@
     tk,
     tv,
     tc,
+    sdq,
+    sdk,
+    tdq,
+    tdk,
+    tdv,
     far,
     raw_s,
     grad_s,
@@ -63,6 +71,8 @@
     sum_frame,
     sum_clip,
     load_sem,
+    spatial_sem,
+    store_sem,
     cross_send,
     mate_send,
     pass_send,
@@ -196,8 +206,20 @@
     def spread(mix, at):
         return jnp.broadcast_to(mix[:, at : at + 1], (block, width))
 
-    def row_part(c):
+    def fold(low, high, body, start):
+        if isinstance(low, int) and isinstance(high, int):
+            for i in range(low, high):
+                start = body(i, start)
+            return start
+        return lax.fori_loop(low, high, body, start)
+
+    def store(which, c):
+        src, dst = ((tdq, tdq_out), (tdk, tdk_out), (tdv, tdv_out))[which]
+        return pltpu.make_async_copy(src.at[rows(c)], dst.at[rows(c)], store_sem.at[which, c])
+
+    def row_part(c, own):
         r = rows(c)
+        known = isinstance(own, int)
         for part in range(2):
             far_here(part, mate, r, c)
             for d in others:
@@ -206,22 +228,34 @@
         raw_own = dots(lambda s: tq[r, s], lambda s: tk[r, s]) * inv
         grad_own = dots(lambda s: tc[r, s], lambda s: tv[r, s])
 
-        @pl.loop(0, me)
-        def _(j):
-            raw_s[j] = dots(lambda s: tq[r, s], lambda s: far[0, j, r, s]) * inv
-            grad_s[j] = dots(lambda s: tc[r, s], lambda s: far[1, j, r, s])
+        def pair(j):
+            return (
+                dots(lambda s: tq[r, s], lambda s: far[0, j, r, s]) * inv,
+                dots(lambda s: tc[r, s], lambda s: far[1, j, r, s]),
+            )
+
+        if known:
+            pairs = [pair(j) for j in range(own)]
+        else:
+
+            @pl.loop(0, own)
+            def _(j):
+                raw_s[j], grad_s[j] = pair(j)
+
+            pairs = [(raw_s[j], grad_s[j]) for j in range(frames - 1)]
+
+        def seen(j, x, other):
+            return x if known else jnp.where(place > j, x, other)
 
         scores_own = raw_own * sharp_lanes
-        raw = [raw_s[j] for j in range(frames - 1)]
-        grad = [grad_s[j] for j in range(frames - 1)]
-        scores = [x * sharp_lanes for x in raw]
+        scores = [x * sharp_lanes for x, _ in pairs]
         top = scores_own
         for j, x in enumerate(scores):
-            top = jnp.maximum(top, jnp.where(place > j, x, scores_own))
+            top = jnp.maximum(top, seen(j, x, scores_own))
         exponent_own = jnp.exp(scores_own - top)
-        exponent = [jnp.where(place > j, jnp.exp(x - top), 0.0) for j, x in enumerate(scores)]
+        exponent = [seen(j, jnp.exp(x - top), 0.0) for j, x in enumerate(scores)]
         total, mean = exponent_own, exponent_own * grad_own
-        for e, g in zip(exponent, grad):
+        for e, (_, g) in zip(exponent, pairs):
             total, mean = total + e, mean + e * g
         over = 1.0 / total
         delta = mean * over
@@ -231,13 +265,13 @@
             score_grad = weights * (g - delta)
             return score_grad, jnp.where(lane < HALF, weights, pltpu.roll(score_grad, HALF, 1)).astype(BF16)
 
-        score_grad, mix = mixed(exponent_own, grad_own)
-        mix_out[me, r] = mix
+        score_grad, mix_own = mixed(exponent_own, grad_own)
+        mix_out[own, r] = mix_own
         share_sum = score_grad * raw_own
 
-        for j in range(frames - 1):
-            score_grad, mix = mixed(exponent[j], grad[j])
-            share_sum = share_sum + score_grad * raw[j]
+        for j, (raw, grad) in enumerate(pairs):
+            score_grad, mix = mixed(exponent[j], grad)
+            share_sum = share_sum + score_grad * raw
 
             def send_mix(j=j, mix=mix):
                 mix_out[j, r] = mix
@@ -245,7 +279,10 @@
                     mix_out.at[j, r], mix_in.at[me, r], mix_send.at[j, c], mix_recv.at[me, c], "frame", j
                 ).start()
 
-            pl.when(j < me)(send_mix)
+            if known:
+                send_mix()
+            else:
+                pl.when(j < own)(send_mix)
 
         logit_rows[...] += share_sum
 
@@ -258,20 +295,23 @@
                     t + spread(mix, HALF + h) * far[0, j, r, cols(h)].astype(F32) for t, h in zip(sums, some)
                 )
 
-            mix = mix_out[me, r].astype(F32)
+            mix = mix_own.astype(F32)
             sums = tuple(spread(mix, HALF + h) * tk[r, cols(h)].astype(F32) for h in some)
-            sums = lax.fori_loop(0, me, add_key, sums)
+            sums = fold(0, own, add_key, sums)
             for t, h in zip(sums, some):
                 tdq[r, cols(h)] = (t * (sharp[1, h] * inv)).astype(BF16)
-
-    def column_part(c):
+        store(0, c).start()
+
+    def column_part(c, own):
         r = rows(c)
 
-        @pl.loop(me + 1, frames)
-        def _(i):
+        def arrived(i, carry):
             remote(
                 mix_out.at[me, r], mix_in.at[i, r], mix_send.at[me, c], mix_recv.at[i, c], "frame", mate
             ).wait_recv()
+            return carry
+
+        fold(own + 1, frames, arrived, 0)
 
         for first in range(0, heads, HEADS_AT_ONCE):
             some = range(first, min(first + HEADS_AT_ONCE, heads))
@@ -286,7 +326,7 @@
                     for (v, k), h in zip(sums, some)
                 )
 
-            mix = mix_out[me, r].astype(F32)
+            mix = mix_out[own, r].astype(F32)
             sums = tuple(
                 (
                     spread(mix, h) * tc[r, cols(h)].astype(F32),
@@ -294,10 +334,19 @@
                 )
                 for h in some
             )
-            sums = lax.fori_loop(me + 1, frames, add_row, sums)
+            sums = fold(own + 1, frames, add_row, sums)
             for (v, k), h in zip(sums, some):
                 tdv[r, cols(h)] = v.astype(BF16)
                 tdk[r, cols(h)] = (k * (sharp[1, h] * inv)).astype(BF16)
+        store(1, c).start()
+        store(2, c).start()
+
+    def as_frame(work, c):
+        if frames > WRITTEN_OUT:
+            work(c, me)
+            return
+        for f in range(frames):
+            pl.when(me == f)(functools.partial(work, c, f))
 
     def share(buffer, send, recv, axis, mine, size):
         for d in range(1, size):
@@ -329,46 +378,66 @@
 
     per_step = -(-heads // CHUNKS)
 
-    @pl.loop(0, CHUNKS)
+    def spatial_stores():
+        return [
+            pltpu.make_async_copy(src, dst, spatial_sem.at[i])
+            for i, (src, dst) in enumerate(((sdq, sdq_out), (sdk, sdk_out)))
+        ]
+
+    def sum_here():
+        per_head = jnp.sum(logit_heads[...], axis=1, keepdims=True)
+        tall = logit_heads.shape[0]
+        own_lane = lax.broadcasted_iota(jnp.int32, (tall, LANES), 0) == lax.broadcasted_iota(
+            jnp.int32, (tall, LANES), 1
+        )
+        spatial_sum = jnp.sum(jnp.where(own_lane, per_head, 0.0), axis=0, keepdims=True)
+        temporal_sum = jnp.sum(logit_rows[...], axis=0, keepdims=True)
+        which = lax.broadcasted_iota(jnp.int32, (8, LANES), 0)
+        sum_frame[me] = jnp.where(which == 0, spatial_sum, jnp.where(which == 1, temporal_sum, 0.0))
+        share(sum_frame, frame_send, frame_recv, "frame", me, frames)
+
+    def sum_frames():
+        sum_clip[clip] = shared(sum_frame, frame_send, frame_recv, "frame", me, frames)
+        share(sum_clip, clip_send, clip_recv, "clip", clip, clips)
+
+    @pl.loop(0, CHUNKS + 2)
     def _(c):
-        for t in range(per_step):
-            h = c * per_step + t
-            if heads % CHUNKS == 0:
-                spatial(h)
-            else:
-                pl.when(h < heads)(functools.partial(spatial, h))
-
-        take(c * SPLIT)
-
-        @pl.when(c >= 1)
-        def _():
-            row_part(c - 1)
+        @pl.when(c < CHUNKS)
+        def _():
+            for t in range(per_step):
+                h = c * per_step + t
+                if heads % CHUNKS == 0:
+                    spatial(h)
+                else:
+                    pl.when(h < heads)(functools.partial(spatial, h))
+            take(c * SPLIT)
+
+        @pl.when(c == CHUNKS - 1)
+        def _():
+            for copy in spatial_stores():
+                copy.start()
+
+        @pl.when((c >= 1) & (c <= CHUNKS))
+        def _():
+            as_frame(row_part, c - 1)
+
+        pl.when(c == CHUNKS)(sum_here)
+        pl.when(c == CHUNKS + 1)(sum_frames)
 
         @pl.when(c >= 2)
         def _():
-            column_part(c - 2)
-
-        take(c * SPLIT + 1)
-
-    row_part(CHUNKS - 1)
-
-    per_head = jnp.sum(logit_heads[...], axis=1, keepdims=True)
-    tall = logit_heads.shape[0]
-    own_lane = lax.broadcasted_iota(jnp.int32, (tall, LANES), 0) == lax.broadcasted_iota(
-        jnp.int32, (tall, LANES), 1
-    )
-    spatial_sum = jnp.sum(jnp.where(own_lane, per_head, 0.0), axis=0, keepdims=True)
-    temporal_sum = jnp.sum(logit_rows[...], axis=0, keepdims=True)
-    which = lax.broadcasted_iota(jnp.int32, (8, LANES), 0)
-    sum_frame[me] = jnp.where(which == 0, spatial_sum, jnp.where(which == 1, temporal_sum, 0.0))
-    share(sum_frame, frame_send, frame_recv, "frame", me, frames)
-    column_part(CHUNKS - 2)
-    sum_clip[clip] = shared(sum_frame, frame_send, frame_recv, "frame", me, frames)
-    share(sum_clip, clip_send, clip_recv, "clip", clip, clips)
-    column_part(CHUNKS - 1)
+            as_frame(column_part, c - 2)
+
+        @pl.when(c < CHUNKS)
+        def _():
+            for p in range(1, SPLIT):
+                take(c * SPLIT + p)
+
     total = shared(sum_clip, clip_send, clip_recv, "clip", clip, clips)
     logit[...] = total[0:2, 0:heads] * scale_norm
 
+    for copy in spatial_stores():
+        copy.wait()
     for d in range(1, frames):
         remote(sum_frame.at[me], sum_frame.at[me], frame_send.at[d], frame_recv.at[me], "frame", mate).wait_send()
     for d in range(1, clips):
@@ -378,6 +447,9 @@
     def _(c):
         for part in range(2):
             far_copy(part, me, rows(c), c, tq_in, mate_send.at[part, c], mate).wait_send()
+
+        for which in range(3):
+            store(which, c).wait()
 
         @pl.loop(0, me)
         def _(j):
@@ -398,9 +470,15 @@
 
 def store_kernel(*refs):
     count = len(refs) // 2
-    copies = [
-        pltpu.make_async_copy(refs[i], refs[count + i], refs[-1].at[i]) for i in range(count)
-    ]
+    sems = refs[-1]
+    copies = []
+    for i in range(count):
+        src, dst = refs[i], refs[count + i]
+        cuts = 2 if src.shape[0] % 32 == 0 else 1
+        tall = src.shape[0] // cuts
+        for part in range(cuts):
+            r = pl.ds(part * tall, tall)
+            copies.append(pltpu.make_async_copy(src.at[r], dst.at[r], sems.at[i, part]))
     for copy in copies:
         copy.start()
     for copy in copies:
@@ -422,9 +500,9 @@
         functools.partial(kernel, frames, clips, heads, scale_norm),
         out_shape=(plane,) * 5 + (jax.ShapeDtypeStruct((2, heads), F32),),
         in_specs=[pl.BlockSpec(memory_space=pltpu.HBM)] * 9,
-        out_specs=(pl.BlockSpec(memory_space=pltpu.VMEM),) * 6,
+        out_specs=(pl.BlockSpec(memory_space=pltpu.HBM),) * OUTPUTS + (pl.BlockSpec(memory_space=pltpu.VMEM),),
         scratch_shapes=[pltpu.SMEM((2, heads), F32)]
-        + [pltpu.VMEM((patches, features), BF16)] * 8
+        + [pltpu.VMEM((patches, features), BF16)] * (8 + OUTPUTS)
         + [
             pltpu.VMEM((2, frames, patches, features), BF16),
             pltpu.VMEM((frames, block, LANES), F32),
@@ -436,6 +514,8 @@
             pltpu.VMEM((frames, 8, LANES), F32),
             pltpu.VMEM((clips, 8, LANES), F32),
             dma((9,)),
+            dma((2,)),
+            dma((3, CHUNKS)),
             dma((2, chips, CHUNKS * SPLIT)),
             dma((2, CHUNKS)),
             dma((2, chips, CHUNKS * SPLIT)),
@@ -448,15 +528,16 @@
             dma((clips,)),
         ],
         compiler_params=pltpu.CompilerParams(
-            collective_id=0, has_side_effects=True, vmem_limit_bytes=32 * 1024 * 1024
+            collective_id=0, has_side_effects=True, vmem_limit_bytes=GRANT
         ),
     )(sharpness, *flat)
     out = pl.pallas_call(
         store_kernel,
         out_shape=(plane,) * 5 + (jax.ShapeDtypeStruct((2, heads), F32),),
-        in_specs=[pl.BlockSpec(memory_space=pltpu.VMEM)] * 6,
+        in_specs=[pl.BlockSpec(memory_space=pltpu.HBM)] * 6,
         out_specs=(pl.BlockSpec(memory_space=pltpu.HBM),) * 6,
-        scratch_shapes=[dma((6,))],
+        scratch_shapes=[dma((6, 2))],
+        compiler_params=pltpu.CompilerParams(vmem_limit_bytes=GRANT),
     )(*out)
     return tuple(x.reshape(full) for x in out[:5]) + (out[5],)
 

time: 53.5 us -> 96.5 us (1.80)
  Pallas kernels: 39.4 us -> 95.7 us
  local copies, waits for them, and re-layouts: 13 us -> 0 us
    pallas_call x1, Pallas kernels: 2.79 us -> 60.8 us  [on_device(): pl.pallas_call(store_kernel, out_shape=(plane,) * 5 + (jax.ShapeDtypeStru...]
    unnamed x30 -> x0, local copies, waits for them, and re-layouts: 13 us -> none
    pallas_call x1, Pallas kernels: 36.6 us -> 34.9 us  [on_device(): pl.pallas_call(functools.partial(kernel, frames, clips, heads, scale_norm...]
where the time goes in v3:
time: 96.5 us; the launch traced here: 96.3 us
  Pallas kernels  95.7 us (99%)
    pallas_call x1, Pallas kernels, on_device(): pl.pallas_call(store_kernel, out_shape=(plane,) * 5 + (jax.ShapeDtypeStru...  60.8 us
    pallas_call x1, Pallas kernels, on_device(): pl.pallas_call(functools.partial(kernel, frames, clips, heads, scale_norm...  34.9 us

profile of v3, /device:TPU:0, one launch (start us, length us, event | category | flops | bytes accessed | tf_op | source)
XLA Modules:
  0.0 96.3 jit_solution(18054714980773631794)
XLA Ops:
  0.6 34.9 %shard_map.136 = (bf16[128,1536]{1,0:T(8,128)(2,1)}, bf16[128,1536]{1,0:T(8,128)(2,1)}, bf16[128,1536]{1,0:T(8,128)(2,1)}, bf16[128,1536]{1,0:T(8,128)(2,1)}, bf...) custom-call(f32[2,12]{1,0:T(2,128)} %sharp_in.1, bf16[128,1536]{1,0:T(8,128)(2,1)} %bitcast.13, bf16[128,1536]{1,0:T(8,128)(2,1)} %bitcast.14, ...), custom_call_target="tpu_custom_call" | custom-call | tf_op jit(solution)/shard_map/pallas_call | solution.py:499
  35.5 60.8 %shard_map.137 = (bf16[128,1536]{1,0:T(8,128)(2,1)}, bf16[128,1536]{1,0:T(8,128)(2,1)}, bf16[128,1536]{1,0:T(8,128)(2,1)}, bf16[128,1536]{1,0:T(8,128)(2,1)}, bf...) custom-call(bf16[128,1536]{1,0:T(8,128)(2,1)} %get-tuple-element.18.refs_0_, bf16[128,1536]{1,0:T(8,128)(2,1)} %get-tuple-element.19.refs_1_, ...), custom_call_target="tpu_custom_call" | custom-call | tf_op jit(solution)/shard_map/pallas_call | solution.py:534

commit v4 on v3

--- a/solution.py
+++ b/solution.py
@@ -14,7 +14,7 @@
 HALF = 64
 CHUNKS = 4
 SPLIT = 2
-AHEAD = 3
+AHEAD = 8
 HEADS_AT_ONCE = 6
 WRITTEN_OUT = 4
 OUTPUTS = 5
@@ -160,7 +160,7 @@
         for d in others:
             send_to(chip_at(d) * 2 + core, piece_rows(p), p, lambda part: cross_send.at[part, d, p])
 
-    for p in range(AHEAD):
+    for p in range(min(AHEAD, pieces)):
         send_far(p)
     for c in range(CHUNKS):
         send_to(mate, rows(c), c, lambda part: mate_send.at[part, c])
@@ -469,20 +469,28 @@
 
 
 def store_kernel(*refs):
-    count = len(refs) // 2
-    sems = refs[-1]
-    copies = []
+    count = (len(refs) - 2) // 3
+    stages, load_sem, save_sem = refs[2 * count : 3 * count], refs[-2], refs[-1]
+    steps = []
     for i in range(count):
-        src, dst = refs[i], refs[count + i]
+        src, dst, stage = refs[i], refs[count + i], stages[i]
         cuts = 2 if src.shape[0] % 32 == 0 else 1
         tall = src.shape[0] // cuts
         for part in range(cuts):
             r = pl.ds(part * tall, tall)
-            copies.append(pltpu.make_async_copy(src.at[r], dst.at[r], sems.at[i, part]))
-    for copy in copies:
-        copy.start()
-    for copy in copies:
-        copy.wait()
+            steps.append(
+                (
+                    pltpu.make_async_copy(src.at[r], stage.at[r], load_sem.at[i, part]),
+                    pltpu.make_async_copy(stage.at[r], dst.at[r], save_sem.at[i, part]),
+                )
+            )
+    for load, _ in steps:
+        load.start()
+    for load, save in steps:
+        load.wait()
+        save.start()
+    for _, save in steps:
+        save.wait()
 
 
 def on_device(sq, sk, sv, sc, tq, tk, tv, tc, sharpness):
@@ -536,7 +544,8 @@
         out_shape=(plane,) * 5 + (jax.ShapeDtypeStruct((2, heads), F32),),
         in_specs=[pl.BlockSpec(memory_space=pltpu.HBM)] * 6,
         out_specs=(pl.BlockSpec(memory_space=pltpu.HBM),) * 6,
-        scratch_shapes=[dma((6, 2))],
+        scratch_shapes=[pltpu.VMEM((patches, features), BF16)] * OUTPUTS
+        + [pltpu.VMEM((2, heads), F32), dma((6, 2)), dma((6, 2))],
         compiler_params=pltpu.CompilerParams(vmem_limit_bytes=GRANT),
     )(*out)
     return tuple(x.reshape(full) for x in out[:5]) + (out[5],)

time: 96.5 us -> 39.5 us (0.41)
  Pallas kernels: 95.7 us -> 38.7 us
    pallas_call x1, Pallas kernels: 60.8 us -> 2.5 us  [on_device(): pl.pallas_call(store_kernel, out_shape=(plane,) * 5 + (jax.ShapeDtypeStru...]
    pallas_call x1, Pallas kernels: 34.9 us -> 36.2 us  [on_device(): pl.pallas_call(functools.partial(kernel, frames, clips, heads, scale_norm...]
where the time goes in v4:
time: 39.5 us; the launch traced here: 39.3 us
  Pallas kernels  38.7 us (98%)
  between operations  0.64 us (2%)
    pallas_call x1, Pallas kernels, on_device(): pl.pallas_call(functools.partial(kernel, frames, clips, heads, scale_norm...  36.2 us
    pallas_call x1, Pallas kernels, on_device(): pl.pallas_call(store_kernel, out_shape=(plane,) * 5 + (jax.ShapeDtypeStru...  2.5 us

profile of v4, /device:TPU:0, one launch (start us, length us, event | category | flops | bytes accessed | tf_op | source)
XLA Modules:
  0.0 39.3 jit_solution(15260643053122875775)
XLA Ops:
  0.6 36.2 %shard_map.136 = (bf16[128,1536]{1,0:T(8,128)(2,1)}, bf16[128,1536]{1,0:T(8,128)(2,1)}, bf16[128,1536]{1,0:T(8,128)(2,1)}, bf16[128,1536]{1,0:T(8,128)(2,1)}, bf...) custom-call(f32[2,12]{1,0:T(2,128)} %sharp_in.1, bf16[128,1536]{1,0:T(8,128)(2,1)} %bitcast.13, bf16[128,1536]{1,0:T(8,128)(2,1)} %bitcast.14, ...), custom_call_target="tpu_custom_call" | custom-call | tf_op jit(solution)/shard_map/pallas_call | solution.py:507
  36.8 2.5 %shard_map.137 = (bf16[128,1536]{1,0:T(8,128)(2,1)}, bf16[128,1536]{1,0:T(8,128)(2,1)}, bf16[128,1536]{1,0:T(8,128)(2,1)}, bf16[128,1536]{1,0:T(8,128)(2,1)}, bf...) custom-call(bf16[128,1536]{1,0:T(8,128)(2,1)} %get-tuple-element.18.refs_0_, bf16[128,1536]{1,0:T(8,128)(2,1)} %get-tuple-element.19.refs_1_, ...), custom_call_target="tpu_custom_call" | custom-call | tf_op jit(solution)/shard_map/pallas_call | solution.py:542

commit v5 on v4

--- a/solution.py
+++ b/solution.py
@@ -12,9 +12,10 @@
 BF16 = jnp.bfloat16
 LANES = 128
 HALF = 64
-CHUNKS = 4
-SPLIT = 2
-AHEAD = 8
+CHUNKS = 8
+SPLIT = 1
+AHEAD = 2
+SPATIAL_STEPS = 4
 HEADS_AT_ONCE = 6
 WRITTEN_OUT = 4
 OUTPUTS = 5
@@ -376,7 +377,7 @@
         def _():
             send_far(p + AHEAD)
 
-    per_step = -(-heads // CHUNKS)
+    per_step = -(-heads // SPATIAL_STEPS)
 
     def spatial_stores():
         return [
@@ -404,15 +405,20 @@
     def _(c):
         @pl.when(c < CHUNKS)
         def _():
-            for t in range(per_step):
-                h = c * per_step + t
-                if heads % CHUNKS == 0:
-                    spatial(h)
-                else:
+            if heads % SPATIAL_STEPS == 0:
+
+                @pl.when(c < SPATIAL_STEPS)
+                def _():
+                    for t in range(per_step):
+                        spatial(c * per_step + t)
+
+            else:
+                for t in range(per_step):
+                    h = c * per_step + t
                     pl.when(h < heads)(functools.partial(spatial, h))
             take(c * SPLIT)
 
-        @pl.when(c == CHUNKS - 1)
+        @pl.when(c == SPATIAL_STEPS)
         def _():
             for copy in spatial_stores():
                 copy.start()

time: 39.5 us -> 41.3 us (1.046)
  Pallas kernels: 38.7 us -> 40.5 us
    pallas_call x1, Pallas kernels: 36.2 us -> 38 us  [on_device(): pl.pallas_call(functools.partial(kernel, frames, clips, heads, scale_norm...]
where the time goes in v5:
time: 41.3 us; the launch traced here: 41.1 us
  Pallas kernels  40.5 us (98%)
  between operations  0.64 us (2%)
    pallas_call x1, Pallas kernels, on_device(): pl.pallas_call(functools.partial(kernel, frames, clips, heads, scale_norm...  38 us
    pallas_call x1, Pallas kernels, on_device(): pl.pallas_call(store_kernel, out_shape=(plane,) * 5 + (jax.ShapeDtypeStru...  2.5 us

profile of v5, /device:TPU:0, one launch (start us, length us, event | category | flops | bytes accessed | tf_op | source)
XLA Modules:
  0.0 41.1 jit_solution(1695654663866591382)
XLA Ops:
  0.6 38.0 %shard_map.136 = (bf16[128,1536]{1,0:T(8,128)(2,1)}, bf16[128,1536]{1,0:T(8,128)(2,1)}, bf16[128,1536]{1,0:T(8,128)(2,1)}, bf16[128,1536]{1,0:T(8,128)(2,1)}, bf...) custom-call(f32[2,12]{1,0:T(2,128)} %sharp_in.1, bf16[128,1536]{1,0:T(8,128)(2,1)} %bitcast.13, bf16[128,1536]{1,0:T(8,128)(2,1)} %bitcast.14, ...), custom_call_target="tpu_custom_call" | custom-call | tf_op jit(solution)/shard_map/pallas_call | solution.py:513
  38.6 2.5 %shard_map.137 = (bf16[128,1536]{1,0:T(8,128)(2,1)}, bf16[128,1536]{1,0:T(8,128)(2,1)}, bf16[128,1536]{1,0:T(8,128)(2,1)}, bf16[128,1536]{1,0:T(8,128)(2,1)}, bf...) custom-call(bf16[128,1536]{1,0:T(8,128)(2,1)} %get-tuple-element.18.refs_0_, bf16[128,1536]{1,0:T(8,128)(2,1)} %get-tuple-element.19.refs_1_, ...), custom_call_target="tpu_custom_call" | custom-call | tf_op jit(solution)/shard_map/pallas_call | solution.py:548

commit v6 on v5

--- a/solution.py
+++ b/solution.py
@@ -12,10 +12,10 @@
 BF16 = jnp.bfloat16
 LANES = 128
 HALF = 64
-CHUNKS = 8
-SPLIT = 1
-AHEAD = 2
-SPATIAL_STEPS = 4
+CHUNKS = 4
+SPLIT = 2
+AHEAD = 3
+SPATIAL_STEPS = 3
 HEADS_AT_ONCE = 6
 WRITTEN_OUT = 4
 OUTPUTS = 5

time: 41.3 us -> 38.2 us (0.925)
  Pallas kernels: 40.5 us -> 37.4 us
    pallas_call x1, Pallas kernels: 38 us -> 34.9 us  [on_device(): pl.pallas_call(functools.partial(kernel, frames, clips, heads, scale_norm...]
where the time goes in v6:
time: 38.2 us; the launch traced here: 38 us
  Pallas kernels  37.4 us (98%)
  between operations  0.64 us (2%)
    pallas_call x1, Pallas kernels, on_device(): pl.pallas_call(functools.partial(kernel, frames, clips, heads, scale_norm...  34.9 us
    pallas_call x1, Pallas kernels, on_device(): pl.pallas_call(store_kernel, out_shape=(plane,) * 5 + (jax.ShapeDtypeStru...  2.5 us

profile of v6, /device:TPU:0, one launch (start us, length us, event | category | flops | bytes accessed | tf_op | source)
XLA Modules:
  0.0 38.0 jit_solution(12891783919289238455)
XLA Ops:
  0.6 34.9 %shard_map.136 = (bf16[128,1536]{1,0:T(8,128)(2,1)}, bf16[128,1536]{1,0:T(8,128)(2,1)}, bf16[128,1536]{1,0:T(8,128)(2,1)}, bf16[128,1536]{1,0:T(8,128)(2,1)}, bf...) custom-call(f32[2,12]{1,0:T(2,128)} %sharp_in.1, bf16[128,1536]{1,0:T(8,128)(2,1)} %bitcast.13, bf16[128,1536]{1,0:T(8,128)(2,1)} %bitcast.14, ...), custom_call_target="tpu_custom_call" | custom-call | tf_op jit(solution)/shard_map/pallas_call | solution.py:513
  35.5 2.5 %shard_map.137 = (bf16[128,1536]{1,0:T(8,128)(2,1)}, bf16[128,1536]{1,0:T(8,128)(2,1)}, bf16[128,1536]{1,0:T(8,128)(2,1)}, bf16[128,1536]{1,0:T(8,128)(2,1)}, bf...) custom-call(bf16[128,1536]{1,0:T(8,128)(2,1)} %get-tuple-element.18.refs_0_, bf16[128,1536]{1,0:T(8,128)(2,1)} %get-tuple-element.19.refs_1_, ...), custom_call_target="tpu_custom_call" | custom-call | tf_op jit(solution)/shard_map/pallas_call | solution.py:548
